TPU v7x, 256 devices: a whole 4x4x8 slice. The times are simulated.
256 devices in a mesh: blk: 32 (over x, z_hi, y), slab: 8 (over z_lo, core).
Axes of the slice: x: 4, y: 4, z: 8 (z_hi: 2, z_lo: 4; z = z_hi * 4 + z_lo), core: 2. Of those that a mesh axis runs over, the one named last changes fastest.
Arguments:
- old_factor: bfloat16 [8192, 98304], P('slab', 'blk'), may hold values from -0.0390625 to 0.0390625
- solved: bfloat16 [98304, 512], P('blk', 'slab'), may hold values from -6 to 6
- band: bfloat16 [8192, 8192], P('blk'), may hold values from -0.0625 to 0.0625
- inv_diag: bfloat16 [2048, 8192], P(None, 'blk'), may hold values from -1 to 2, as said below
- rhs: bfloat16 [8192, 512], P('blk', 'slab'), may hold values from -6 to 6
Outputs:
- solution: bfloat16 [8192, 512], P('blk', 'slab')
Inputs may be any that keep to these rules, and one draw needn't show every extreme that they name: `inv_diag`: columns k * 2048 to (k + 1) * 2048 - 1 hold the inverse applied in block step k.
All inputs are finite; a program needn't handle non-finite values.
Results may differ from a plain program's by a relative error of at most 0.008.
Values may be sent and summed in bfloat16 or wider, within the bound.
No kernel may reach another device: no remote copies, remote signals or barrier semaphores. Data moves between devices by JAX's collectives and lax.ppermute only.
A program may use at most 64 MiB of HBM per device.

v0:
```python
import jax
import jax.numpy as jnp
from jax import lax
from jax.sharding import PartitionSpec as P

STEPS = 4


def body(old_factor, solved, band, inv_diag, rhs):
    own_rows = rhs.shape[0]
    block_rows = inv_diag.shape[0]
    group_size = block_rows // own_rows
    own_index = lax.axis_index("blk")
    own_block = own_index // group_size
    offset = own_index % group_size * own_rows
    partial_value = jnp.dot(
        old_factor,
        lax.all_gather(solved, "slab", axis=1, tiled=True),
        preferred_element_type=jnp.float32,
    )
    window_terms = lax.all_to_all(partial_value, "slab", split_axis=1, concat_axis=0, tiled=True)
    source = rhs.astype(jnp.float32)
    accum = jnp.zeros(rhs.shape, jnp.float32)
    solution = jnp.zeros(rhs.shape, jnp.bfloat16)
    for step in range(STEPS):
        current = window_terms[step * block_rows : (step + 1) * block_rows, :]
        summed = lax.psum(current, "blk")
        total = accum + lax.dynamic_slice_in_dim(summed, offset, own_rows, 0)
        resid = (source - total).astype(jnp.bfloat16)
        term = jnp.dot(inv_diag, resid, preferred_element_type=jnp.float32)
        term = jnp.where(own_block == step, term, jnp.zeros_like(term))
        newest = lax.psum(term, "blk").astype(jnp.bfloat16)
        mine = lax.dynamic_slice_in_dim(newest, offset, own_rows, 0)
        solution = jnp.where(own_block == step, mine, solution)
        if step + 1 < STEPS:
            columns = band[:, step * block_rows : (step + 1) * block_rows]
            update = jnp.dot(columns, newest, preferred_element_type=jnp.float32)
            accum = accum + jnp.where(own_block > step, update, jnp.zeros_like(update))
    return solution


def solution(mesh):
    return jax.shard_map(
        body,
        mesh=mesh,
        in_specs=(
            P("slab", "blk"),
            P("blk", "slab"),
            P("blk", None),
            P(None, "blk"),
            P("blk", "slab"),
        ),
        out_specs=P("blk", "slab"),
        check_vma=False,
    )
```

profile of v0, /device:TPU:32, one launch (start us, length us, event | category | flops | bytes accessed | tf_op | source)
XLA Modules:
  0.0 1458.0 jit_solution(7909967818730247592)
XLA Ops:
  6.5 0.0 copy-start
  6.5 0.0 all-gather.2.cloned.1.call-start
  6.5 0.7 all-gather.2.cloned.1.call-update
  7.3 0.0 all-reduce.7.cloned.1.call-start
  7.3 45.2 %all-gather.2.cloned.1.call-done = bf16[3072,512]{0,1:T(8,128)(2,1)} async-done(((bf16[3072,64]{0,1:T(8,128)(2,1)}), bf16[3072,512]{0,1:T(8,128)(2,1)}) %all-gather.2.cloned.1.call-update) | async-done | bytes 3145744 | tf_op jit(solution)/shard_map/all_gather | solution.py:18
  52.5 6.5 fusion.32
  59.0 53.8 %all_to_all.16 = f32[1024,8,64]{0,2,1:T(8,128)S(1)} all-to-all(f32[1024,8,64]{0,2,1:T(8,128)S(1)} %bitcast.50), channel_id=1, replica_groups=mesh['blk'=32,'slab'=8] {'slab'}, dimensions={1} | all-to-all | bytes 4194304 | tf_op jit(solution)/shard_map/all_to_all | solution.py:21
  112.8 0.2 slice_bitcast_fusion
  113.1 0.0 copy-start.1
  113.1 0.8 copy.10
  113.9 0.8 copy.11
  114.8 0.8 copy.12
  115.6 0.8 copy.13
  116.4 0.0 all-reduce.7.cloned.1.call-update
  116.5 434.7 %all-reduce.7.cloned.1.call-done = (f32[2048,64]{0,1:T(8,128)}, f32[2048,64]{0,1:T(8,128)}, f32[2048,64]{0,1:T(8,128)}, f32[2048,64]{0,1:T(8,128)}) async-done(((f32[2048,64]{0,1:T(8,128)}, f32[2048,64]{0,1:T(8,128)}, f32[2048,64]{0,1:T(8,128)}, f32[2048,64]{0,1:T(8,128)}), (f32[2048,64]{0,1:T(8,128)}, f32[2048,64]{0,1:T(8,128)}, f32[2048,64]{0,1:T(8,128)}, ...) | async-done | bytes 2097168 | tf_op jit(solution)/shard_map/psum | solution.py:27
  551.2 0.0 copy-done
  551.2 0.0 copy-done.1
  551.2 1.3 fusion
  552.5 229.7 %all-reduce.8 = bf16[2048,64]{0,1:T(8,128)(2,1)S(1)} all-reduce(f32[2048,64]{0,1:T(8,128)S(1)} %fusion), channel_id=1, replica_groups=mesh['blk'=32,'slab'=8] {'blk'}, use_global_device_ids=true, to_apply=%region_1.2 | all-reduce | flops 131072 | bytes 786432 | tf_op jit(solution)/shard_map/psum | solution.py:32
  782.2 1.7 fusion.10
  783.9 1.3 fusion.1
  785.2 219.4 %all-reduce.9 = bf16[2048,64]{0,1:T(8,128)(2,1)S(1)} all-reduce(f32[2048,64]{0,1:T(8,128)S(1)} %fusion.1), channel_id=1, replica_groups=mesh['blk'=32,'slab'=8] {'blk'}, use_global_device_ids=true, to_apply=%region_3.4 | all-reduce | flops 131072 | bytes 786432 | tf_op jit(solution)/shard_map/psum | solution.py:32
  1004.5 1.7 fusion.9
  1006.2 1.3 fusion.2
  1007.5 221.2 %all-reduce.10 = bf16[2048,64]{0,1:T(8,128)(2,1)S(1)} all-reduce(f32[2048,64]{0,1:T(8,128)S(1)} %fusion.2), channel_id=1, replica_groups=mesh['blk'=32,'slab'=8] {'blk'}, use_global_device_ids=true, to_apply=%region_5.6 | all-reduce | flops 131072 | bytes 786432 | tf_op jit(solution)/shard_map/psum | solution.py:32
  1228.7 2.5 fusion.3
  1231.2 219.3 %all-reduce.11 = bf16[2048,64]{0,1:T(8,128)(2,1)S(1)} all-reduce(f32[2048,64]{0,1:T(8,128)S(1)} %fusion.3), channel_id=1, replica_groups=mesh['blk'=32,'slab'=8] {'blk'}, use_global_device_ids=true, to_apply=%region_7.8 | all-reduce | flops 131072 | bytes 786432 | tf_op jit(solution)/shard_map/psum | solution.py:32
  1450.5 0.6 fusion.21
Async XLA Ops:
  6.5 544.7 %copy-start = (bf16[2048,256]{1,0:T(8,128)(2,1)S(1)}, bf16[2048,256]{1,0:T(8,128)(2,1)}, u32[]{:S(2)}) copy-start(bf16[2048,256]{1,0:T(8,128)(2,1)} %param.8) | copy-start | bytes 3145732
  6.5 46.0 %all-gather.2.cloned.1.call-start = ((), (), s32[]{:S(2)}) async-start(), calls=%async_computation.1 | async-start | bytes 3538944 | tf_op jit(solution)/shard_map/all_gather | solution.py:18
  7.3 543.9 %all-reduce.7.cloned.1.call-start = ((), (), s32[]{:S(2)}) async-start(), calls=%async_computation.2 | async-start | bytes 4194304 | tf_op jit(solution)/shard_map/psum | solution.py:27
  113.1 438.1 %copy-start.1 = (bf16[256,64]{0,1:T(8,128)(2,1)S(1)}, bf16[256,64]{0,1:T(8,128)(2,1)}, u32[]{:S(2)}) copy-start(bf16[256,64]{0,1:T(8,128)(2,1)} %param.9) | copy-start | bytes 98308
Sparse Core Ops, SparseCore 0:
  9.1 43.3 all-gather.1
  116.6 434.5 all-reduce.6
where the time goes:
time: 1460 us
  blocking collectives  943 us (65%)
  waiting for transfers between devices  481 us (33%)
  matrix products  16.2 us (1%)
    psum x4, blocking collectives, body(): newest = lax.psum(term, 'blk').astype(jnp.bfloat16)  890 us
    psum x1, waiting for transfers between devices, body(): summed = lax.psum(current, 'blk')  435 us
    all_to_all x1, blocking collectives, body(): lax.all_to_all(partial_value, 'slab', split_axis=1, concat_axis=0, tiled=...  53.8 us
    all_gather x1, waiting for transfers between devices, body(): lax.all_gather(solved, 'slab', axis=1, tiled=True)  45.2 us
  transfers between devices with their start and end apart: 2, of which 2 were waited for; matrix products, arithmetic and copies ran while one was open for 0% of the time, Pallas kernels for 0%

commit v1 on v0

v1 whole, which is shorter than its diff:
```python
import jax
import jax.numpy as jnp
from jax import lax
from jax.sharding import Mesh, PartitionSpec as P

STEPS = 4
SHAPE = (4, 2, 4, 4, 2)
AXES = ("x", "zh", "y", "zl", "core")
BLK = ("x", "zh", "y")
SLAB = ("zl", "core")
F32, BF16 = jnp.float32, jnp.bfloat16


def position(x, zh, y, zl, core):
    return (((x * 2 + zh) * 4 + y) * 4 + zl) * 2 + core


def moves(target):
    pairs = []
    for x in range(4):
        for zh in range(2):
            for y in range(4):
                for zl in range(4):
                    for core in range(2):
                        to = target(x, zh, y, zl, core)
                        if to is not None:
                            pairs.append((position(x, zh, y, zl, core), position(*to)))
    return pairs


def permute(array, target):
    return lax.ppermute(array, AXES, moves(target))


def swap_core(array):
    return lax.ppermute(array, "core", [(0, 1), (1, 0)])


def mirrored(first_plane):
    return lambda x, zh, y, zl, core: (x, 1 - zh, y, 3 - zl, core) if x >= first_plane else None


def mul_t(left, right):
    return lax.dot_general(left, right, (((1,), (1,)), ((), ())), preferred_element_type=F32)


def by_core(core, mine, other):
    return jnp.where(core == 0, jnp.concatenate([mine, other], 1), jnp.concatenate([other, mine], 1))


def body(old_factor, solved, band, inv_diag, rhs):
    zh = lax.axis_index("zh")
    core = lax.axis_index("core")
    depth, own_columns = solved.shape
    rows = rhs.shape[0]
    nb = inv_diag.shape[0]
    half = own_columns // 2

    mine = solved.T
    parts = [mine] + [
        lax.ppermute(mine, "zl", [(i, (i + d) % 4) for i in range(4)]) for d in (1, 2, 3)
    ]
    far_inverse = permute(lax.dynamic_slice_in_dim(inv_diag, core * (nb // 2), nb // 2, 0), mirrored(0))
    far_inverse2 = swap_core(far_inverse)
    far_band = []
    for k in range(STEPS - 1):
        piece = lax.dynamic_slice(band, (core * (rows // 2), k * nb), (rows // 2, nb))
        piece = permute(piece, mirrored(k + 1))
        far_band.append((piece, swap_core(piece)))

    gathered = jnp.stack([jnp.stack([p, swap_core(p)]) for p in parts])
    gathered = gathered.reshape(4 * 2 * own_columns, depth)
    partial = mul_t(gathered, old_factor).astype(BF16)
    partial = partial.reshape(4, 2, 2, half, 4, rows).transpose(0, 2, 4, 1, 3, 5)
    partial = partial.reshape(32, 2 * half, rows)
    summed = lax.all_to_all(partial, BLK, 0, 0, tiled=True).astype(F32).sum(0)
    kept, sent = summed[:half], summed[half:]
    other = swap_core(sent)
    earlier = by_core(core, kept, other)
    earlier = permute(earlier, lambda x, zh, y, zl, core: (zl, zh, y, (zl - x) % 4, core))

    source = rhs.T
    mine_half = jnp.where(zh == 0, source[:half], source[half:])
    sent_half = jnp.where(zh == 0, source[half:], source[:half])
    far_source = lax.ppermute(sent_half, "zh", [(0, 1), (1, 0)])
    near = mine_half.astype(F32) - jnp.where(zh == 0, earlier[:, :rows], earlier[:, rows:])
    far = far_source.astype(F32) - jnp.where(zh == 0, earlier[:, rows:], earlier[:, :rows])

    def product():
        resid_near, resid_far = near.astype(BF16), far.astype(BF16)
        value = mul_t(resid_near, inv_diag)
        value = value + by_core(core, mul_t(resid_far, far_inverse), mul_t(resid_far, far_inverse2))
        return value.astype(BF16)

    known = []
    for k in range(STEPS - 1):
        term = product()
        pieces = [
            permute(
                term,
                lambda x, zh, y, zl, core, d=d: (x + 1, zh, (y + d) % 4, zl, core) if x == k else None,
            )
            for d in range(4)
        ]
        newest = sum(p.astype(F32) for p in pieces).astype(BF16)
        for hop in range(2, STEPS - k):
            newest = newest + permute(
                newest,
                lambda x, zh, y, zl, core, hop=hop: (k + hop, zh, y, zl, core) if x == k + 1 else None,
            )
        columns = band[:, k * nb : (k + 1) * nb]
        later = lax.axis_index("x") > k
        near = near - jnp.where(later, mul_t(newest, columns), 0.0)
        far = far - jnp.where(later, by_core(core, mul_t(newest, far_band[k][0]), mul_t(newest, far_band[k][1])), 0.0)

    term = product().reshape(half, 8, rows).transpose(1, 0, 2)
    term = lax.all_to_all(term, ("zh", "y"), 0, 0, tiled=True)
    out = term.reshape(2, 4, half, rows).astype(F32).sum(1).reshape(2 * half, rows)
    return out.astype(BF16).T


def solution(mesh):
    fine = Mesh(mesh.devices.reshape(SHAPE), AXES)
    return jax.shard_map(
        body,
        mesh=fine,
        in_specs=(
            P(SLAB, BLK),
            P(BLK, SLAB),
            P(BLK, None),
            P(None, BLK),
            P(BLK, SLAB),
        ),
        out_specs=P(BLK, SLAB),
        check_vma=False,
    )
```

time: 1460 us -> 232 us (0.16)
  the two profiles are of different devices: /device:TPU:32 before, /device:TPU:102 now
where the time goes in v1:
time: 232 us; the launch traced here: 230 us
  waiting for transfers between devices  146 us (63%)
  starting transfers between devices  37.4 us (16%)
  blocking collectives  20.6 us (9%)
  matrix products  16.3 us (7%)
  local copies, waits for them, and re-layouts  5.61 us (2%)
  other arithmetic  3.02 us (1%)
    ppermute x20, waiting for transfers between devices, permute(): return lax.ppermute(array, AXES, moves(target))  85.6 us
    ppermute x3, waiting for transfers between devices, body(): lax.ppermute(mine, 'zl', [(i, (i + d) % 4) for i in range(4)])  33.9 us
    all_to_all x1, waiting for transfers between devices, body(): summed = lax.all_to_all(partial, BLK, 0, 0, tiled=True).astype(F32).sum(0)  25.6 us
    ppermute x20, starting transfers between devices, permute(): return lax.ppermute(array, AXES, moves(target))  22 us
    all_to_all x1, blocking collectives, body(): term = lax.all_to_all(term, ('zh', 'y'), 0, 0, tiled=True)  20.6 us
    dot_general x21, matrix products, mul_t(): lax.dot_general(left, right, (((1,), (1,)), ((), ())), preferred_element_...  16.3 us
    all_to_all x1, starting transfers between devices, body(): summed = lax.all_to_all(partial, BLK, 0, 0, tiled=True).astype(F32).sum(0)  12.5 us
  transfers between devices with their start and end apart: 34, of which 15 were waited for; matrix products, arithmetic and copies ran while one was open for 6% of the time, Pallas kernels for 0%

profile of v1, /device:TPU:102, one launch (start us, length us, event | category | flops | bytes accessed | tf_op | source)
XLA Modules:
  0.0 229.7 jit_solution(14737156347365066909)
XLA Ops:
  0.0 1.6 collective-permute-start.3
  1.6 0.5 collective-permute-start.5
  2.0 9.4 %collective-permute-done.1 = bf16[64,3072]{1,0:T(8,128)(2,1)S(1)} collective-permute-done((bf16[64,3072]{1,0:T(8,128)(2,1)}, bf16[64,3072]{1,0:T(8,128)(2,1)S(1)}, u32[]{:S(2)}, u32[]{:S(2)}) %collective-permute-start.1) | collective-permute-done | bytes 393248 | tf_op jit(solution)/shard_map/ppermute | solution.py:61
  11.5 24.4 %collective-permute-done.3 = bf16[64,3072]{1,0:T(8,128)(2,1)S(1)} collective-permute-done((bf16[64,3072]{1,0:T(8,128)(2,1)}, bf16[64,3072]{1,0:T(8,128)(2,1)S(1)}, u32[]{:S(2)}, u32[]{:S(2)}) %collective-permute-start.3) | collective-permute-done | bytes 393248 | tf_op jit(solution)/shard_map/ppermute | solution.py:61
  35.9 1.2 maximum_bitcast_fusion
  37.1 0.6 collective-permute-start.6
  37.9 1.2 collective-permute-done.6
  39.2 0.4 pad_maximum_fusion
  39.6 1.0 slice-done.1
  40.7 3.5 %convolution_convert_fusion = bf16[512,1024]{1,0:T(8,128)(2,1)S(1)} fusion(bf16[512,3072]{1,0:T(8,128)(2,1)S(1)} %bitcast.60, bf16[1024,3072]{1,0:T(8,128)(2,1)S(1)} %bitcast.78), kind=kOutput, calls=%fused_computation.4 | convolution fusion | flops 3221749760 | bytes 10485760 | tf_op jit(solution)/shard_map/dot_general | solution.py:44
  44.2 0.8 reshape.18
  45.0 1.2 copy.10
  46.1 12.5 %all-to-all-start = ((bf16[32,64,256]{2,1,0:T(8,128)(2,1)}), bf16[32,64,256]{2,1,0:T(8,128)(2,1)S(1)}, u32[]{:S(2)}, u32[]{:S(2)}) async-start(bf16[32,64,256]{2,1,0:T(8,128)(2,1)} %bitcast.16), calls=%async_computation | async-start | bytes 2097152 | tf_op jit(solution)/shard_map/all_to_all | solution.py:76
  58.8 25.6 %all-to-all-done = bf16[32,64,256]{2,1,0:T(8,128)(2,1)S(1)} async-done(((bf16[32,64,256]{2,1,0:T(8,128)(2,1)}), bf16[32,64,256]{2,1,0:T(8,128)(2,1)S(1)}, u32[]{:S(2)}, u32[]{:S(2)}) %all-to-all-start) | async-done | bytes 1048608 | tf_op jit(solution)/shard_map/all_to_all | solution.py:76
  84.8 23.2 %collective-permute-done.10 = bf16[1024,256]{1,0:T(8,128)(2,1)S(1)} collective-permute-done((bf16[1024,256]{1,0:T(8,128)(2,1)S(1)}, bf16[1024,256]{1,0:T(8,128)(2,1)S(1)}, u32[]{:S(2)}, u32[]{:S(2)}) %collective-permute-start.10) | collective-permute-done | bytes 524320 | tf_op jit(solution)/shard_map/ppermute | solution.py:32
  108.0 1.9 collective-permute-start.8
  109.9 2.5 %constant_dynamic-slice_fusion = (bf16[128,2048]{1,0:T(8,128)(2,1)}, bf16[128,2048]{1,0:T(8,128)(2,1)}, bf16[128,2048]{1,0:T(8,128)(2,1)S(1)}) fusion(bf16[256,8192]{1,0:T(8,128)(2,1)} %param.7, s32[]{:T(128)S(6)} %select_n.118), kind=kLoop, calls=%fused_computation.68 | loop fusion | bytes 3145732 | tf_op jit(solution)/shard_map/dynamic_slice | solution.py:67
  112.4 1.9 collective-permute-start.18
  114.4 1.2 collective-permute-done.8
  115.9 0.3 fusion.42
  116.1 0.4 fusion
  116.6 0.8 collective-permute-start.12
  117.4 0.7 collective-permute-start.13
  118.1 0.7 collective-permute-start.14
  118.8 0.7 collective-permute-start.15
  119.5 21.6 %collective-permute-done.18 = bf16[128,2048]{1,0:T(8,128)(2,1)S(1)} collective-permute-done((bf16[128,2048]{1,0:T(8,128)(2,1)S(1)}, bf16[128,2048]{1,0:T(8,128)(2,1)S(1)}, u32[]{:S(2)}, u32[]{:S(2)}) %collective-permute-start.18) | collective-permute-done | bytes 524320 | tf_op jit(solution)/shard_map/ppermute | solution.py:32
  141.2 0.7 collective-permute-start.16
  142.0 1.3 collective-permute-start.17
  143.3 2.2 collective-permute-start.25
  145.5 7.2 %collective-permute-done.17 = bf16[32,2048]{1,0:T(8,128)(2,1)S(1)} collective-permute-done((bf16[32,2048]{1,0:T(8,128)(2,1)S(1)}, bf16[32,2048]{1,0:T(8,128)(2,1)S(1)}, u32[]{:S(2)}, u32[]{:S(2)}) %collective-permute-start.17) | collective-permute-done | bytes 131104 | tf_op jit(solution)/shard_map/ppermute | solution.py:32
  152.6 0.3 fusion.54
  152.9 1.3 fusion.52
  154.3 1.6 fusion.3
  155.9 0.2 fusion.40
  156.2 0.3 fusion.38
  156.4 0.4 fusion.13
  156.9 0.7 collective-permute-start.20
  157.5 0.7 collective-permute-start.21
  158.2 0.7 collective-permute-start.22
  158.9 0.7 collective-permute-start.23
  159.6 16.8 %collective-permute-done.25 = bf16[128,2048]{1,0:T(8,128)(2,1)S(1)} collective-permute-done((bf16[128,2048]{1,0:T(8,128)(2,1)}, bf16[128,2048]{1,0:T(8,128)(2,1)S(1)}, u32[]{:S(2)}, u32[]{:S(2)}) %collective-permute-start.25) | collective-permute-done | bytes 524320 | tf_op jit(solution)/shard_map/ppermute | solution.py:32
  176.5 1.3 collective-permute-start.24
  177.8 1.9 collective-permute-start.31
  179.8 4.5 %collective-permute-done.24 = bf16[32,2048]{1,0:T(8,128)(2,1)S(1)} collective-permute-done((bf16[32,2048]{1,0:T(8,128)(2,1)S(1)}, bf16[32,2048]{1,0:T(8,128)(2,1)S(1)}, u32[]{:S(2)}, u32[]{:S(2)}) %collective-permute-start.24) | collective-permute-done | bytes 131104 | tf_op jit(solution)/shard_map/ppermute | solution.py:32
  184.3 0.3 fusion.49
  184.6 1.3 fusion.47
  185.9 1.7 fusion.2
  187.8 0.3 fusion.34
  188.1 0.4 fusion.15
  188.5 1.3 collective-permute-start.27
  189.8 1.3 collective-permute-start.28
  191.1 1.3 collective-permute-start.29
  192.4 1.3 collective-permute-start.30
  193.7 1.7 collective-permute-done.31
  195.4 0.7 collective-permute-done.27
  196.1 5.7 %collective-permute-done.28 = bf16[32,2048]{1,0:T(8,128)(2,1)S(1)} collective-permute-done((bf16[32,2048]{1,0:T(8,128)(2,1)S(1)}, bf16[32,2048]{1,0:T(8,128)(2,1)S(1)}, u32[]{:S(2)}, u32[]{:S(2)}) %collective-permute-start.28) | collective-permute-done | bytes 131104 | tf_op jit(solution)/shard_map/ppermute | solution.py:32
  201.8 2.6 %collective-permute-done.29 = bf16[32,2048]{1,0:T(8,128)(2,1)S(1)} collective-permute-done((bf16[32,2048]{1,0:T(8,128)(2,1)S(1)}, bf16[32,2048]{1,0:T(8,128)(2,1)S(1)}, u32[]{:S(2)}, u32[]{:S(2)}) %collective-permute-start.29) | collective-permute-done | bytes 131104 | tf_op jit(solution)/shard_map/ppermute | solution.py:32
  204.4 0.3 collective-permute-done.30
  204.8 0.3 fusion.58
  205.1 0.3 fusion.59
  205.7 0.3 fusion.61
  206.0 2.5 %fusion.7 = bf16[32,2048]{1,0:T(8,128)(2,1)S(1)} fusion(bf16[2048,256]{1,0:T(8,128)(2,1)S(1)} %copy-done, f32[32,256]{1,0:T(8,128)S(1)} %fusion.2, bf16[32,2048]{1,0:T(8,128)(2,1)S(1)} %add_convert_fusion, bf16[256,8192]{1,0:T(8,128)(2,1)} %param.7, f32[32,1024]{1,0:T(8,128)S(1)} %fusion.61, f32[32,1024]{1,0:T(8,128)S(1)} %fusion.60, pred[]{:T(512)S(6)} %eq.5, ...), kind=kOutput, calls=%fused_computation.14 | convolution fusion | flops 67461120 | bytes 2654210 | tf_op jit(solution)/shard_map/dot_general | solution.py:44
  208.5 20.6 %all_to_all.10 = bf16[8,32,256]{2,1,0:T(8,128)(2,1)S(1)} all-to-all(bf16[8,32,256]{2,1,0:T(8,128)(2,1)S(1)} %bitcast.62), channel_id=1, replica_groups=mesh['x'=4,'zh'=2,'y'=4,'zl'=4,'core'=2] {'zh','y'}, dimensions={0} | all-to-all | bytes 262144 | tf_op jit(solution)/shard_map/all_to_all | solution.py:117
  229.1 0.6 bitcast_reduce_fusion
  (58 shorter events, 2.0 us)
Async XLA Ops:
  0.0 58.6 %copy-start = (bf16[2048,256]{1,0:T(8,128)(2,1)S(1)}, bf16[2048,256]{1,0:T(8,128)(2,1)}, u32[]{:S(2)}) copy-start(bf16[2048,256]{1,0:T(8,128)(2,1)} %param.8) | copy-start | bytes 3145732
  0.0 11.5 %collective-permute-start.1 = (bf16[64,3072]{1,0:T(8,128)(2,1)}, bf16[64,3072]{1,0:T(8,128)(2,1)S(1)}, u32[]{:S(2)}, u32[]{:S(2)}) collective-permute-start(bf16[64,3072]{1,0:T(8,128)(2,1)} %bitcast.63), channel_id=1, source_target_pairs={{0,2},{2,4},{4,6},{6,0},{1,3},{3,5},{5,7},{7,1},{8,10},{10,12},{12... | collective-permute-start | bytes 1179656 | tf_op jit(solution)/shard_map/ppermute | solution.py:61
  0.0 35.9 %collective-permute-start.3 = (bf16[64,3072]{1,0:T(8,128)(2,1)}, bf16[64,3072]{1,0:T(8,128)(2,1)S(1)}, u32[]{:S(2)}, u32[]{:S(2)}) collective-permute-start(bf16[64,3072]{1,0:T(8,128)(2,1)} %bitcast.64), channel_id=1, source_target_pairs={{0,4},{2,6},{4,0},{6,2},{1,5},{3,7},{5,1},{7,3},{8,12},{10,14},{12... | collective-permute-start | bytes 1179656 | tf_op jit(solution)/shard_map/ppermute | solution.py:61
  1.6 34.3 %collective-permute-start = (bf16[64,3072]{1,0:T(8,128)(2,1)}, bf16[64,3072]{1,0:T(8,128)(2,1)S(1)}, u32[]{:S(2)}, u32[]{:S(2)}) collective-permute-start(bf16[64,3072]{1,0:T(8,128)(2,1)} %bitcast.65), channel_id=1, source_target_pairs={{0,1},{1,0},{2,3},{3,2},{4,5},{5,4},{6,7},{7,6},{8,9},{9,8},{10,11... | collective-permute-start | bytes 1179656 | tf_op jit(solution)/shard_map/ppermute | solution.py:36
  1.6 35.6 %collective-permute-start.5 = (bf16[64,3072]{1,0:T(8,128)(2,1)}, bf16[64,3072]{1,0:T(8,128)(2,1)S(1)}, u32[]{:S(2)}, u32[]{:S(2)}) collective-permute-start(bf16[64,3072]{1,0:T(8,128)(2,1)} %bitcast.66), channel_id=1, source_target_pairs={{0,6},{2,0},{4,2},{6,4},{1,7},{3,1},{5,3},{7,5},{8,14},{10,8},{12,... | collective-permute-start | bytes 1179656 | tf_op jit(solution)/shard_map/ppermute | solution.py:61
  11.5 26.3 %collective-permute-start.2 = (bf16[64,3072]{1,0:T(8,128)(2,1)S(1)}, bf16[64,3072]{1,0:T(8,128)(2,1)S(1)}, u32[]{:S(2)}, u32[]{:S(2)}) collective-permute-start(bf16[64,3072]{1,0:T(8,128)(2,1)S(1)} %collective-permute-done.1), channel_id=1, source_target_pairs={{0,1},{1,0},{2,3},{3,2},{4,5},{5,4},{6,7},{7,6},{8,9},{9,8},{10,11... | collective-permute-start | bytes 1179656 | tf_op jit(solution)/shard_map/ppermute | solution.py:36
  35.9 1.9 collective-permute-start.4
  35.9 3.7 %slice-start = ((s8[6291456]{0:T(1024)(128)(4,1)}), s8[4194304]{0:T(1024)(128)(4,1)S(1)}, s32[]{:S(2)}) async-start(s8[6291456]{0:T(1024)(128)(4,1)} %bitcast.77), calls=%async_computation.2 | async-start | bytes 8388608
  37.1 1.9 collective-permute-start.6
  39.1 1.6 slice-start.1
  44.1 40.5 %copy-start.1 = (bf16[256,64]{0,1:T(8,128)(2,1)S(1)}, bf16[256,64]{0,1:T(8,128)(2,1)}, u32[]{:S(2)}) copy-start(bf16[256,64]{0,1:T(8,128)(2,1)} %param.9) | copy-start | bytes 98308
  46.1 38.3 %all-to-all-start = ((bf16[32,64,256]{2,1,0:T(8,128)(2,1)}), bf16[32,64,256]{2,1,0:T(8,128)(2,1)S(1)}, u32[]{:S(2)}, u32[]{:S(2)}) async-start(bf16[32,64,256]{2,1,0:T(8,128)(2,1)} %bitcast.16), calls=%async_computation | async-start | bytes 2097152 | tf_op jit(solution)/shard_map/all_to_all | solution.py:76
  58.7 49.3 %collective-permute-start.10 = (bf16[1024,256]{1,0:T(8,128)(2,1)S(1)}, bf16[1024,256]{1,0:T(8,128)(2,1)S(1)}, u32[]{:S(2)}, u32[]{:S(2)}) collective-permute-start(bf16[1024,256]{1,0:T(8,128)(2,1)S(1)} %constant_dynamic-slice_fusion.2), channel_id=1, source_target_pairs={{0,38},{1,39},{2,36},{3,37},{4,34},{5,35},{6,32},{7,33},{8,46},{9,... | collective-permute-start | bytes 1572872 | tf_op jit(solution)/shard_map/ppermute | solution.py:32
  84.6 23.4 %collective-permute-start.7 = (f32[32,256]{1,0:T(8,128)S(1)}, f32[32,256]{1,0:T(8,128)S(1)}, u32[]{:S(2)}, u32[]{:S(2)}) collective-permute-start(f32[32,256]{1,0:T(8,128)S(1)} %get-tuple-element.11), channel_id=1, source_target_pairs={{0,1},{1,0},{2,3},{3,2},{4,5},{5,4},{6,7},{7,6},{8,9},{9,8},{10,11... | collective-permute-start | bytes 98312 | tf_op jit(solution)/shard_map/ppermute | solution.py:36
  84.7 29.7 %collective-permute-start.9 = (bf16[32,256]{1,0:T(8,128)(2,1)S(1)}, bf16[32,256]{1,0:T(8,128)(2,1)S(1)}, u32[]{:S(2)}, u32[]{:S(2)}) collective-permute-start(bf16[32,256]{1,0:T(8,128)(2,1)S(1)} %broadcast_select_fusion), channel_id=1, source_target_pairs={{0,32},{32,0},{1,33},{33,1},{2,34},{34,2},{3,35},{35,3},{4,36},{36... | collective-permute-start | bytes 49160 | tf_op jit(solution)/shard_map/ppermute | solution.py:85
  108.0 7.9 %collective-permute-start.11 = (bf16[1024,256]{1,0:T(8,128)(2,1)S(1)}, bf16[1024,256]{1,0:T(8,128)(2,1)S(1)}, u32[]{:S(2)}, u32[]{:S(2)}) collective-permute-start(bf16[1024,256]{1,0:T(8,128)(2,1)S(1)} %collective-permute-done.10), channel_id=1, source_target_pairs={{0,1},{1,0},{2,3},{3,2},{4,5},{5,4},{6,7},{7,6},{8,9},{9,8},{10,11... | collective-permute-start | bytes 1572872 | tf_op jit(solution)/shard_map/ppermute | solution.py:36
  108.0 7.6 %collective-permute-start.8 = (f32[32,512]{1,0:T(8,128)S(1)}, f32[32,512]{1,0:T(8,128)S(1)}, u32[]{:S(2)}, u32[]{:S(2)}) collective-permute-start(f32[32,512]{1,0:T(8,128)S(1)} %maximum_select_fusion.4), channel_id=1, source_target_pairs={{0,0},{1,1},{2,66},{3,67},{4,132},{5,133},{6,198},{7,199},{8,8},{9... | collective-permute-start | bytes 196616 | tf_op jit(solution)/shard_map/ppermute | solution.py:32
  112.4 28.7 %collective-permute-start.18 = (bf16[128,2048]{1,0:T(8,128)(2,1)S(1)}, bf16[128,2048]{1,0:T(8,128)(2,1)S(1)}, u32[]{:S(2)}, u32[]{:S(2)}) collective-permute-start(bf16[128,2048]{1,0:T(8,128)(2,1)S(1)} %get-tuple-element.7), channel_id=1, source_target_pairs={{64,102},{65,103},{66,100},{67,101},{68,98},{69,99},{70,96},{71,97... | collective-permute-start | bytes 1572872 | tf_op jit(solution)/shard_map/ppermute | solution.py:32
  116.6 24.5 %collective-permute-start.12 = (bf16[32,2048]{1,0:T(8,128)(2,1)S(1)}, bf16[32,2048]{1,0:T(8,128)(2,1)S(1)}, u32[]{:S(2)}, u32[]{:S(2)}) collective-permute-start(bf16[32,2048]{1,0:T(8,128)(2,1)S(1)} %fusion), channel_id=1, source_target_pairs={{0,64},{1,65},{2,66},{3,67},{4,68},{5,69},{6,70},{7,71},{8,72},{9,... | collective-permute-start | bytes 393224 | tf_op jit(solution)/shard_map/ppermute | solution.py:32
  117.4 23.7 %collective-permute-start.13 = (bf16[32,2048]{1,0:T(8,128)(2,1)S(1)}, bf16[32,2048]{1,0:T(8,128)(2,1)S(1)}, u32[]{:S(2)}, u32[]{:S(2)}) collective-permute-start(bf16[32,2048]{1,0:T(8,128)(2,1)S(1)} %fusion), channel_id=1, source_target_pairs={{0,72},{1,73},{2,74},{3,75},{4,76},{5,77},{6,78},{7,79},{8,80},{9,... | collective-permute-start | bytes 393224 | tf_op jit(solution)/shard_map/ppermute | solution.py:32
  118.1 23.0 %collective-permute-start.14 = (bf16[32,2048]{1,0:T(8,128)(2,1)S(1)}, bf16[32,2048]{1,0:T(8,128)(2,1)S(1)}, u32[]{:S(2)}, u32[]{:S(2)}) collective-permute-start(bf16[32,2048]{1,0:T(8,128)(2,1)S(1)} %fusion), channel_id=1, source_target_pairs={{0,80},{1,81},{2,82},{3,83},{4,84},{5,85},{6,86},{7,87},{8,88},{9,... | collective-permute-start | bytes 393224 | tf_op jit(solution)/shard_map/ppermute | solution.py:32
  118.8 22.3 %collective-permute-start.15 = (bf16[32,2048]{1,0:T(8,128)(2,1)S(1)}, bf16[32,2048]{1,0:T(8,128)(2,1)S(1)}, u32[]{:S(2)}, u32[]{:S(2)}) collective-permute-start(bf16[32,2048]{1,0:T(8,128)(2,1)S(1)} %fusion), channel_id=1, source_target_pairs={{0,88},{1,89},{2,90},{3,91},{4,92},{5,93},{6,94},{7,95},{8,64},{9,... | collective-permute-start | bytes 393224 | tf_op jit(solution)/shard_map/ppermute | solution.py:32
  141.1 11.8 %collective-permute-start.19 = (bf16[128,2048]{1,0:T(8,128)(2,1)S(1)}, bf16[128,2048]{1,0:T(8,128)(2,1)}, u32[]{:S(2)}, u32[]{:S(2)}) collective-permute-start(bf16[128,2048]{1,0:T(8,128)(2,1)S(1)} %collective-permute-done.18), channel_id=1, source_target_pairs={{0,1},{1,0},{2,3},{3,2},{4,5},{5,4},{6,7},{7,6},{8,9},{9,8},{10,11... | collective-permute-start | bytes 1572872 | tf_op jit(solution)/shard_map/ppermute | solution.py:36
  141.2 0.7 collective-permute-start.16
  142.0 10.7 %collective-permute-start.17 = (bf16[32,2048]{1,0:T(8,128)(2,1)S(1)}, bf16[32,2048]{1,0:T(8,128)(2,1)S(1)}, u32[]{:S(2)}, u32[]{:S(2)}) collective-permute-start(bf16[32,2048]{1,0:T(8,128)(2,1)S(1)} %add.61), channel_id=1, source_target_pairs={{64,192},{65,193},{66,194},{67,195},{68,196},{69,197},{70,198},{71... | collective-permute-start | bytes 393224 | tf_op jit(solution)/shard_map/ppermute | solution.py:32
  143.3 33.1 %collective-permute-start.25 = (bf16[128,2048]{1,0:T(8,128)(2,1)}, bf16[128,2048]{1,0:T(8,128)(2,1)S(1)}, u32[]{:S(2)}, u32[]{:S(2)}) collective-permute-start(bf16[128,2048]{1,0:T(8,128)(2,1)} %get-tuple-element.6), channel_id=1, source_target_pairs={{128,166},{129,167},{130,164},{131,165},{132,162},{133,163},{134,1... | collective-permute-start | bytes 1572872 | tf_op jit(solution)/shard_map/ppermute | solution.py:32
  156.9 19.6 %collective-permute-start.20 = (bf16[32,2048]{1,0:T(8,128)(2,1)S(1)}, bf16[32,2048]{1,0:T(8,128)(2,1)S(1)}, u32[]{:S(2)}, u32[]{:S(2)}) collective-permute-start(bf16[32,2048]{1,0:T(8,128)(2,1)S(1)} %fusion.13), channel_id=1, source_target_pairs={{64,128},{65,129},{66,130},{67,131},{68,132},{69,133},{70,134},{71... | collective-permute-start | bytes 393224 | tf_op jit(solution)/shard_map/ppermute | solution.py:32
  157.5 18.9 %collective-permute-start.21 = (bf16[32,2048]{1,0:T(8,128)(2,1)S(1)}, bf16[32,2048]{1,0:T(8,128)(2,1)S(1)}, u32[]{:S(2)}, u32[]{:S(2)}) collective-permute-start(bf16[32,2048]{1,0:T(8,128)(2,1)S(1)} %fusion.13), channel_id=1, source_target_pairs={{64,136},{65,137},{66,138},{67,139},{68,140},{69,141},{70,142},{71... | collective-permute-start | bytes 393224 | tf_op jit(solution)/shard_map/ppermute | solution.py:32
  158.2 18.2 %collective-permute-start.22 = (bf16[32,2048]{1,0:T(8,128)(2,1)S(1)}, bf16[32,2048]{1,0:T(8,128)(2,1)S(1)}, u32[]{:S(2)}, u32[]{:S(2)}) collective-permute-start(bf16[32,2048]{1,0:T(8,128)(2,1)S(1)} %fusion.13), channel_id=1, source_target_pairs={{64,144},{65,145},{66,146},{67,147},{68,148},{69,149},{70,150},{71... | collective-permute-start | bytes 393224 | tf_op jit(solution)/shard_map/ppermute | solution.py:32
  158.9 17.5 %collective-permute-start.23 = (bf16[32,2048]{1,0:T(8,128)(2,1)S(1)}, bf16[32,2048]{1,0:T(8,128)(2,1)S(1)}, u32[]{:S(2)}, u32[]{:S(2)}) collective-permute-start(bf16[32,2048]{1,0:T(8,128)(2,1)S(1)} %fusion.13), channel_id=1, source_target_pairs={{64,152},{65,153},{66,154},{67,155},{68,156},{69,157},{70,158},{71... | collective-permute-start | bytes 393224 | tf_op jit(solution)/shard_map/ppermute | solution.py:32
  176.4 8.2 %collective-permute-start.26 = (bf16[128,2048]{1,0:T(8,128)(2,1)S(1)}, bf16[128,2048]{1,0:T(8,128)(2,1)}, u32[]{:S(2)}, u32[]{:S(2)}) collective-permute-start(bf16[128,2048]{1,0:T(8,128)(2,1)S(1)} %collective-permute-done.25), channel_id=1, source_target_pairs={{0,1},{1,0},{2,3},{3,2},{4,5},{5,4},{6,7},{7,6},{8,9},{9,8},{10,11... | collective-permute-start | bytes 1572872 | tf_op jit(solution)/shard_map/ppermute | solution.py:36
  176.5 7.7 %collective-permute-start.24 = (bf16[32,2048]{1,0:T(8,128)(2,1)S(1)}, bf16[32,2048]{1,0:T(8,128)(2,1)S(1)}, u32[]{:S(2)}, u32[]{:S(2)}) collective-permute-start(bf16[32,2048]{1,0:T(8,128)(2,1)S(1)} %add_convert_fusion.1), channel_id=1, source_target_pairs={{128,192},{129,193},{130,194},{131,195},{132,196},{133,197},{134,1... | collective-permute-start | bytes 393224 | tf_op jit(solution)/shard_map/ppermute | solution.py:32
  177.8 17.6 %collective-permute-start.31 = (bf16[128,2048]{1,0:T(8,128)(2,1)}, bf16[128,2048]{1,0:T(8,128)(2,1)S(1)}, u32[]{:S(2)}, u32[]{:S(2)}) collective-permute-start(bf16[128,2048]{1,0:T(8,128)(2,1)} %get-tuple-element.5), channel_id=1, source_target_pairs={{192,230},{193,231},{194,228},{195,229},{196,226},{197,227},{198,2... | collective-permute-start | bytes 1572872 | tf_op jit(solution)/shard_map/ppermute | solution.py:32
  188.5 7.6 %collective-permute-start.27 = (bf16[32,2048]{1,0:T(8,128)(2,1)S(1)}, bf16[32,2048]{1,0:T(8,128)(2,1)S(1)}, u32[]{:S(2)}, u32[]{:S(2)}) collective-permute-start(bf16[32,2048]{1,0:T(8,128)(2,1)S(1)} %fusion.15), channel_id=1, source_target_pairs={{128,192},{129,193},{130,194},{131,195},{132,196},{133,197},{134,1... | collective-permute-start | bytes 393224 | tf_op jit(solution)/shard_map/ppermute | solution.py:32
  189.8 12.0 %collective-permute-start.28 = (bf16[32,2048]{1,0:T(8,128)(2,1)S(1)}, bf16[32,2048]{1,0:T(8,128)(2,1)S(1)}, u32[]{:S(2)}, u32[]{:S(2)}) collective-permute-start(bf16[32,2048]{1,0:T(8,128)(2,1)S(1)} %fusion.15), channel_id=1, source_target_pairs={{128,200},{129,201},{130,202},{131,203},{132,204},{133,205},{134,2... | collective-permute-start | bytes 393224 | tf_op jit(solution)/shard_map/ppermute | solution.py:32
  191.1 13.3 %collective-permute-start.29 = (bf16[32,2048]{1,0:T(8,128)(2,1)S(1)}, bf16[32,2048]{1,0:T(8,128)(2,1)S(1)}, u32[]{:S(2)}, u32[]{:S(2)}) collective-permute-start(bf16[32,2048]{1,0:T(8,128)(2,1)S(1)} %fusion.15), channel_id=1, source_target_pairs={{128,208},{129,209},{130,210},{131,211},{132,212},{133,213},{134,2... | collective-permute-start | bytes 393224 | tf_op jit(solution)/shard_map/ppermute | solution.py:32
  192.4 12.4 %collective-permute-start.30 = (bf16[32,2048]{1,0:T(8,128)(2,1)S(1)}, bf16[32,2048]{1,0:T(8,128)(2,1)S(1)}, u32[]{:S(2)}, u32[]{:S(2)}) collective-permute-start(bf16[32,2048]{1,0:T(8,128)(2,1)S(1)} %fusion.15), channel_id=1, source_target_pairs={{128,216},{129,217},{130,218},{131,219},{132,220},{133,221},{134,2... | collective-permute-start | bytes 393224 | tf_op jit(solution)/shard_map/ppermute | solution.py:32
  195.4 9.7 %collective-permute-start.32 = (bf16[128,2048]{1,0:T(8,128)(2,1)S(1)}, bf16[128,2048]{1,0:T(8,128)(2,1)S(1)}, u32[]{:S(2)}, u32[]{:S(2)}) collective-permute-start(bf16[128,2048]{1,0:T(8,128)(2,1)S(1)} %collective-permute-done.31), channel_id=1, source_target_pairs={{0,1},{1,0},{2,3},{3,2},{4,5},{5,4},{6,7},{7,6},{8,9},{9,8},{10,11... | collective-permute-start | bytes 1572872 | tf_op jit(solution)/shard_map/ppermute | solution.py:36

commit v2 on v1

v2 whole, which is shorter than its diff:
```python
import jax
import jax.numpy as jnp
from jax import lax
from jax.experimental import pallas as pl
from jax.experimental.pallas import tpu as pltpu
from jax.sharding import Mesh, PartitionSpec as P

STEPS = 4
SHAPE = (4, 2, 4, 4, 2)
AXES = ("x", "zh", "y", "zl", "core")
BLK = ("x", "zh", "y")
SLAB = ("zl", "core")
F32, BF16 = jnp.float32, jnp.bfloat16


def position(x, zh, y, zl, core):
    return (((x * 2 + zh) * 4 + y) * 4 + zl) * 2 + core


def moves(target):
    pairs = []
    for x in range(4):
        for zh in range(2):
            for y in range(4):
                for zl in range(4):
                    for core in range(2):
                        to = target(x, zh, y, zl, core)
                        if to is not None:
                            pairs.append((position(x, zh, y, zl, core), position(*to)))
    return pairs


def permute(array, target):
    return lax.ppermute(array, AXES, moves(target))


def swap_core(array):
    return lax.ppermute(array, "core", [(0, 1), (1, 0)])


def other_half(first_plane):
    return lambda x, zh, y, zl, core: (x, 1 - zh, y, zl, core) if x >= first_plane else None


def by_core(core, mine, other):
    return jnp.where(core == 0, jnp.concatenate([mine, other], 1), jnp.concatenate([other, mine], 1))


def mul_t(left, right):
    return lax.dot_general(left, right, (((1,), (1,)), ((), ())), preferred_element_type=F32)


def partial_kernel(*refs):
    parts, factor, out, columns = refs[:8], refs[8], refs[9], refs[10]
    width = parts[0].shape[0]

    @pl.when(pl.program_id(0) == 0)
    def _():
        for i, part in enumerate(parts):
            columns[i * width : (i + 1) * width, :] = part[...]

    out[...] = mul_t(columns[...], factor[...]).astype(BF16).reshape(out.shape)


def partial_products(parts, factor, rows):
    width, depth = parts[0].shape
    groups = factor.shape[0] // rows
    return pl.pallas_call(
        partial_kernel,
        grid=(groups,),
        in_specs=[pl.BlockSpec((width, depth), lambda i: (0, 0))] * 8
        + [pl.BlockSpec((rows, depth), lambda i: (i, 0))],
        out_specs=pl.BlockSpec((4, 1, 2 * width, rows), lambda i: (0, i, 0, 0)),
        out_shape=jax.ShapeDtypeStruct((4, groups, 2 * width, rows), BF16),
        scratch_shapes=[pltpu.VMEM((8 * width, depth), BF16)],
        compiler_params=pltpu.CompilerParams(vmem_limit_bytes=56 * 2**20),
    )(*parts, factor)


def term_of(core, near, far, inverse, far_mine, far_other, out, total):
    size = far_mine.shape[0]
    near, far = near.astype(BF16), far.astype(BF16)
    total[...] = mul_t(near, inverse[...])
    for at, part in ((core, far_mine), (1 - core, far_other)):
        place = pl.ds(pl.multiple_of(at * size, size), size)
        total[:, place] += mul_t(far, part[...])
    out[...] = total[...].astype(BF16)


def first_kernel(core_ref, near, far, inverse, far_mine, far_other, out, total):
    term_of(core_ref[0], near[...], far[...], inverse, far_mine, far_other, out, total)


def step_kernel(
    core_ref, q0, q1, q2, q3, near, far, band, band_mine, band_other, inverse, far_mine, far_other,
    near_out, far_out, whole, out, total,
):
    core = core_ref[0]
    size = band_mine.shape[0]
    newest = q0[...].astype(F32) + q1[...].astype(F32) + q2[...].astype(F32) + q3[...].astype(F32)
    newest = newest.astype(BF16)
    whole[...] = newest
    near_out[...] = near[...] - mul_t(newest, band[...])
    far_out[...] = far[...]
    for at, part in ((core, band_mine), (1 - core, band_other)):
        place = pl.ds(pl.multiple_of(at * size, size), size)
        far_out[:, place] -= mul_t(newest, part[...])
    term_of(core, near_out[...], far_out[...], inverse, far_mine, far_other, out, total)


SMEM = pl.BlockSpec(memory_space=pltpu.SMEM)
VMEM = pl.BlockSpec(memory_space=pltpu.VMEM)


def body(old_factor, solved, band, inv_diag, rhs):
    zh = lax.axis_index("zh")
    core = lax.axis_index("core")
    core_arr = core.astype(jnp.int32).reshape(1)
    depth, own_columns = solved.shape
    rows = rhs.shape[0]
    nb = inv_diag.shape[0]
    half = own_columns // 2

    slices = [
        lax.dynamic_slice(band, (core * (rows // 2), k * nb), (rows // 2, nb)) for k in range(STEPS - 1)
    ]
    half_inverse = lax.dynamic_slice_in_dim(inv_diag, core * (nb // 2), nb // 2, 0)
    source = rhs.T
    sent_half = jnp.where(zh == 0, source[half:], source[:half])
    mine_half = jnp.where(zh == 0, source[:half], source[half:])
    far_source = lax.ppermute(sent_half, "zh", [(0, 1), (1, 0)])

    mine = solved.T
    parts = [
        lax.ppermute(mine, "zl", [(i, (i + d) % 4) for i in range(4)]) for d in (1, 2, 3)
    ]
    mine, slices, half_inverse, far_source = lax.optimization_barrier((mine, slices, half_inverse, far_source))
    pairs = [q for p in [mine] + parts for q in (p, swap_core(p))]
    pairs, half_inverse = lax.optimization_barrier((pairs, half_inverse))
    far_inverse = permute(half_inverse, other_half(0))

    partial = partial_products(pairs, old_factor, rows)
    partial = partial.reshape(16, 2 * own_columns, rows)
    summed = lax.all_to_all(partial, ("x", "y"), 0, 0, tiled=True).astype(F32).sum(0)
    summed, far_inverse = lax.optimization_barrier((summed, far_inverse))
    far_inverse2 = swap_core(far_inverse)
    other = swap_core(summed[own_columns:])
    both = by_core(core, summed[:own_columns], other)
    stay = jnp.where(zh == 0, both[:half], both[half:])
    leave = jnp.where(zh == 0, both[half:], both[:half])
    stay = permute(stay, lambda x, zh, y, zl, core: (zl, zh, y, (zl - x) % 4, core))
    leave = permute(leave, lambda x, zh, y, zl, core: (zl, 1 - zh, y, (zl - x) % 4, core))
    stay, leave, slices = lax.optimization_barrier((stay, leave, slices))
    earlier = stay + leave

    near = mine_half.astype(F32) - jnp.where(zh == 0, earlier[:, :rows], earlier[:, rows:])
    far = far_source.astype(F32) - jnp.where(zh == 0, earlier[:, rows:], earlier[:, :rows])

    params = pltpu.CompilerParams(vmem_limit_bytes=24 * 2**20)
    whole_shape = jax.ShapeDtypeStruct((half, nb), BF16)
    scratch = [pltpu.VMEM((half, nb), F32)]
    term = pl.pallas_call(
        first_kernel,
        in_specs=[SMEM] + [VMEM] * 5,
        out_specs=VMEM,
        out_shape=whole_shape,
        scratch_shapes=scratch,
        compiler_params=params,
    )(core_arr, near, far, inv_diag, far_inverse, far_inverse2)
    passed = []
    far_band = None
    for k in range(STEPS - 1):
        following = slices[k]
        if far_band is not None:
            following, _ = lax.optimization_barrier((following, far_band))
        before = far_band
        far_band = permute(following, other_half(k + 1))
        far_band2 = swap_core(far_band)
        pieces = [
            permute(
                term,
                lambda x, zh, y, zl, core, d=d: (x + 1, zh, (y + d) % 4, zl, core) if x == k else None,
            )
            for d in range(4)
        ]
        if passed:
            late = sum(passed)
            near = near - mul_t(late, band[:, (k - 1) * nb : k * nb])
            far = far - by_core(core, mul_t(late, before), mul_t(late, before2))
        near, far, whole, term = pl.pallas_call(
            step_kernel,
            grid=(1,),
            in_specs=[SMEM]
            + [VMEM] * 6
            + [pl.BlockSpec((rows, nb), lambda i, k=k: (0, k))]
            + [VMEM] * 5,
            out_specs=[VMEM] * 4,
            out_shape=[
                jax.ShapeDtypeStruct(near.shape, F32),
                jax.ShapeDtypeStruct(far.shape, F32),
                whole_shape,
                whole_shape,
            ],
            scratch_shapes=scratch,
            compiler_params=params,
        )(core_arr, *pieces, near, far, band, far_band, far_band2, inv_diag, far_inverse, far_inverse2)
        before2 = far_band2
        passed = [
            permute(
                whole,
                lambda x, zh, y, zl, core, hop=hop: (k + hop, zh, y, zl, core) if x == k + 1 else None,
            )
            for hop in range(2, STEPS - k)
        ]

    term = term.reshape(half, 8, rows).transpose(1, 0, 2)
    term = lax.all_to_all(term, ("zh", "y"), 0, 0, tiled=True)
    out = term.reshape(2, 4, half, rows).astype(F32).sum(1).reshape(2 * half, rows)
    return out.astype(BF16).T


def solution(mesh):
    fine = Mesh(mesh.devices.reshape(SHAPE), AXES)
    return jax.shard_map(
        body,
        mesh=fine,
        in_specs=(
            P(SLAB, BLK),
            P(BLK, SLAB),
            P(BLK, None),
            P(None, BLK),
            P(BLK, SLAB),
        ),
        out_specs=P(BLK, SLAB),
        check_vma=False,
    )
```

time: 232 us -> 209 us (0.901)
  waiting for transfers between devices: 146 us -> 100 us
  starting transfers between devices: 37.4 us -> 63.6 us
  matrix products: 16.3 us -> 1.93 us
  Pallas kernels: 0 us -> 13.3 us
  blocking collectives: 20.6 us -> 18.1 us
    ppermute x3, waiting for transfers between devices: 33.9 us -> 2.9 us  [body(): lax.ppermute(mine, 'zl', [(i, (i + d) % 4) for i in range(4)])]
    ppermute x20 -> x21, starting transfers between devices: 22 us -> 46.9 us  [permute(): return lax.ppermute(array, AXES, moves(target))]
    ppermute x20 -> x21, waiting for transfers between devices: 85.6 us -> 63 us  [permute(): return lax.ppermute(array, AXES, moves(target))]
    ppermute x1, waiting for transfers between devices: 0.01 us -> 20.8 us  [body(): far_source = lax.ppermute(sent_half, 'zh', [(0, 1), (1, 0)])]
    all_to_all x1, waiting for transfers between devices: 25.6 us -> 10.3 us  [body(): lax.all_to_all(partial, ('x', 'y'), 0, 0, tiled=True).astype(F32).sum(0)]
    dot_general x21 -> x6, matrix products: 16.3 us -> 1.93 us  [mul_t(): lax.dot_general(left, right, (((1,), (1,)), ((), ())), preferred_element_...]
    pallas_call x0 -> x5, Pallas kernels: none -> 13.3 us  [the longest x1 7.92 us: partial_products(): pl.pallas_call(partial_kernel, grid=(groups,), in_specs=[pl.BlockSpec((wi...]
    ppermute x1, starting transfers between devices: 0.13 us -> 5.94 us  [body(): far_source = lax.ppermute(sent_half, 'zh', [(0, 1), (1, 0)])]
  transfers between devices with their start and end apart: 34 -> 35, of which waited for: 15 -> 18; matrix products, arithmetic and copies ran while one was open for 6% -> 3% of each run, Pallas kernels for 0% -> 2%
where the time goes in v2:
time: 209 us; the launch traced here: 206 us
  waiting for transfers between devices  100 us (48%)
  starting transfers between devices  63.6 us (30%)
  blocking collectives  18.1 us (9%)
  Pallas kernels  13.3 us (6%)
  local copies, waits for them, and re-layouts  6.77 us (3%)
    ppermute x21, waiting for transfers between devices, permute(): return lax.ppermute(array, AXES, moves(target))  63 us
    ppermute x21, starting transfers between devices, permute(): return lax.ppermute(array, AXES, moves(target))  46.9 us
    ppermute x1, waiting for transfers between devices, body(): far_source = lax.ppermute(sent_half, 'zh', [(0, 1), (1, 0)])  20.8 us
    all_to_all x1, blocking collectives, body(): term = lax.all_to_all(term, ('zh', 'y'), 0, 0, tiled=True)  18.1 us
    all_to_all x1, waiting for transfers between devices, body(): lax.all_to_all(partial, ('x', 'y'), 0, 0, tiled=True).astype(F32).sum(0)  10.3 us
    pallas_call x1, Pallas kernels, partial_products(): pl.pallas_call(partial_kernel, grid=(groups,), in_specs=[pl.BlockSpec((wi...  7.92 us
    all_to_all x1, starting transfers between devices, body(): lax.all_to_all(partial, ('x', 'y'), 0, 0, tiled=True).astype(F32).sum(0)  7.56 us
    ppermute x1, starting transfers between devices, body(): far_source = lax.ppermute(sent_half, 'zh', [(0, 1), (1, 0)])  5.94 us
  transfers between devices with their start and end apart: 35, of which 18 were waited for; matrix products, arithmetic and copies ran while one was open for 3% of the time, Pallas kernels for 2%

profile of v2, /device:TPU:102, one launch (start us, length us, event | category | flops | bytes accessed | tf_op | source)
XLA Modules:
  0.0 206.0 jit_solution(13146520495883031499)
XLA Ops:
  0.0 1.6 collective-permute-start.4
  1.6 0.5 collective-permute-start.6
  2.0 0.7 broadcast_select_fusion
  2.8 5.9 %collective-permute-start = (bf16[32,256]{1,0:T(8,128)(2,1)S(1)}, bf16[32,256]{1,0:T(8,128)(2,1)S(1)}, u32[]{:S(2)}, u32[]{:S(2)}) collective-permute-start(bf16[32,256]{1,0:T(8,128)(2,1)S(1)} %broadcast_select_fusion), channel_id=1, source_target_pairs={{0,32},{32,0},{1,33},{33,1},{2,34},{34,2},{3,35},{35,3},{4,36},{36... | collective-permute-start | bytes 49160 | tf_op jit(solution)/shard_map/ppermute | solution.py:131
  8.7 2.6 %constant_dynamic-slice_fusion = (bf16[128,2048]{1,0:T(8,128)(2,1)}, bf16[128,2048]{1,0:T(8,128)(2,1)}, bf16[128,2048]{1,0:T(8,128)(2,1)}) fusion(bf16[256,8192]{1,0:T(8,128)(2,1)} %band.5, s32[]{:T(128)S(6)} %select_n.64), kind=kLoop, calls=%fused_computation.17 | loop fusion | bytes 3145732 | tf_op jit(solution)/shard_map/dynamic_slice | solution.py:125
  11.3 1.1 constant_dynamic-slice_fusion.1
  12.4 20.8 %collective-permute-done = bf16[32,256]{1,0:T(8,128)(2,1)S(1)} collective-permute-done((bf16[32,256]{1,0:T(8,128)(2,1)S(1)}, bf16[32,256]{1,0:T(8,128)(2,1)S(1)}, u32[]{:S(2)}, u32[]{:S(2)}) %collective-permute-start) | collective-permute-done | bytes 16416 | tf_op jit(solution)/shard_map/ppermute | solution.py:131
  33.2 0.5 collective-permute-start.3
  33.7 2.9 %collective-permute-done.4.refs_4_ = bf16[64,3072]{1,0:T(8,128)(2,1)S(1)} collective-permute-done((bf16[64,3072]{1,0:T(8,128)(2,1)}, bf16[64,3072]{1,0:T(8,128)(2,1)S(1)}, u32[]{:S(2)}, u32[]{:S(2)}) %collective-permute-start.4) | collective-permute-done | bytes 393248 | tf_op jit(solution)/shard_map/ppermute | solution.py:135
  36.6 0.5 collective-permute-start.7
  37.1 1.2 collective-permute-done.5.refs_5_
  38.3 0.6 collective-permute-done.7.refs_7_
  38.9 0.1 copy-done.9
  39.1 0.7 copy-done.10
  39.8 7.9 %shard_map.55 = bf16[4,4,128,256]{3,2,1,0:T(8,128)(2,1)} custom-call(bf16[64,3072]{1,0:T(8,128)(2,1)} %bitcast.29, bf16[64,3072]{1,0:T(8,128)(2,1)} %copy-done.7, bf16[64,3072]{1,0:T(8,128)(2,1)} %copy-done.4, bf16[64,3072]{1,0:T(8,128)(2,1)} %copy-done.8, bf16[64,3072]{1,0:T(8,128)(2,1)} %copy-done.5, bf16[64,3072]{1,0:T(8,128)(2,1)} %copy-done.9, ...), custom_call_target="tpu_custom_call" | custom-call | tf_op jit(solution)/shard_map/pallas_call | solution.py:68
  47.7 7.6 %all-to-all-start = ((bf16[16,128,256]{2,1,0:T(8,128)(2,1)}), bf16[16,128,256]{2,1,0:T(8,128)(2,1)S(1)}, u32[]{:S(2)}, u32[]{:S(2)}) async-start(bf16[16,128,256]{2,1,0:T(8,128)(2,1)} %bitcast.24), calls=%async_computation | async-start | bytes 2097152 | tf_op jit(solution)/shard_map/all_to_all | solution.py:144
  55.3 5.4 %collective-permute-start.8 = (bf16[1024,256]{1,0:T(8,128)(2,1)S(1)}, bf16[1024,256]{1,0:T(8,128)(2,1)S(1)}, u32[]{:S(2)}, u32[]{:S(2)}) collective-permute-start(bf16[1024,256]{1,0:T(8,128)(2,1)S(1)} %constant_dynamic-slice_fusion.1), channel_id=1, source_target_pairs={{0,32},{1,33},{2,34},{3,35},{4,36},{5,37},{6,38},{7,39},{8,40},{9,... | collective-permute-start | bytes 1572872 | tf_op jit(solution)/shard_map/ppermute | solution.py:34
  60.7 10.3 %all-to-all-done = bf16[16,128,256]{2,1,0:T(8,128)(2,1)S(1)} async-done(((bf16[16,128,256]{2,1,0:T(8,128)(2,1)}), bf16[16,128,256]{2,1,0:T(8,128)(2,1)S(1)}, u32[]{:S(2)}, u32[]{:S(2)}) %all-to-all-start) | async-done | bytes 1048608 | tf_op jit(solution)/shard_map/all_to_all | solution.py:144
  71.0 0.1 convert_reduce_fusion
  71.1 3.6 %collective-permute-done.8.far_mine = bf16[1024,256]{1,0:T(8,128)(2,1)S(1)} collective-permute-done((bf16[1024,256]{1,0:T(8,128)(2,1)S(1)}, bf16[1024,256]{1,0:T(8,128)(2,1)S(1)}, u32[]{:S(2)}, u32[]{:S(2)}) %collective-permute-start.8) | collective-permute-done | bytes 524320 | tf_op jit(solution)/shard_map/ppermute | solution.py:34
  74.9 1.2 collective-permute-done.9
  76.1 1.9 collective-permute-start.10
  78.1 14.3 %collective-permute-start.11 = (f32[32,512]{1,0:T(8,128)S(1)}, f32[32,512]{1,0:T(8,128)S(1)}, u32[]{:S(2)}, u32[]{:S(2)}) collective-permute-start(f32[32,512]{1,0:T(8,128)S(1)} %get-tuple-element.74), channel_id=1, source_target_pairs={{0,32},{1,33},{2,98},{3,99},{4,164},{5,165},{6,230},{7,231},{8,40}... | collective-permute-start | bytes 196616 | tf_op jit(solution)/shard_map/ppermute | solution.py:34
  92.4 1.9 collective-permute-done.11
  94.3 2.3 %collective-permute-start.17 = (bf16[128,2048]{1,0:T(8,128)(2,1)}, bf16[128,2048]{1,0:T(8,128)(2,1)S(1)}, u32[]{:S(2)}, u32[]{:S(2)}) collective-permute-start(bf16[128,2048]{1,0:T(8,128)(2,1)} %get-tuple-element.57), channel_id=1, source_target_pairs={{64,96},{65,97},{66,98},{67,99},{68,100},{69,101},{70,102},{71,103... | collective-permute-start | bytes 1572872 | tf_op jit(solution)/shard_map/ppermute | solution.py:34
  96.6 16.8 %collective-permute-done.17.band_mine = bf16[128,2048]{1,0:T(8,128)(2,1)S(1)} collective-permute-done((bf16[128,2048]{1,0:T(8,128)(2,1)}, bf16[128,2048]{1,0:T(8,128)(2,1)S(1)}, u32[]{:S(2)}, u32[]{:S(2)}) %collective-permute-start.17) | collective-permute-done | bytes 524320 | tf_op jit(solution)/shard_map/ppermute | solution.py:34
  113.4 3.1 %collective-permute-start.25 = (bf16[128,2048]{1,0:T(8,128)(2,1)}, bf16[128,2048]{1,0:T(8,128)(2,1)S(1)}, u32[]{:S(2)}, u32[]{:S(2)}) collective-permute-start(bf16[128,2048]{1,0:T(8,128)(2,1)} %get-tuple-element.63), channel_id=1, source_target_pairs={{128,160},{129,161},{130,162},{131,163},{132,164},{133,165},{134,1... | collective-permute-start | bytes 1572872 | tf_op jit(solution)/shard_map/ppermute | solution.py:34
  116.6 0.7 shard_map.56
  117.4 0.7 collective-permute-start.13
  118.1 0.7 collective-permute-start.14
  118.7 0.7 collective-permute-start.15
  119.4 0.7 collective-permute-start.16
  120.2 2.2 %copy-done = bf16[256,8192]{1,0:T(8,128)(2,1)S(1)} copy-done((bf16[256,8192]{1,0:T(8,128)(2,1)S(1)}, bf16[256,8192]{1,0:T(8,128)(2,1)}, u32[]{:S(2)}) %copy-start) | copy-done | bytes 4194328
  122.3 1.4 shard_map.57
  123.7 0.7 collective-permute-start.23
  124.4 1.3 collective-permute-start.24
  125.7 0.7 collective-permute-start.19
  126.4 0.7 collective-permute-start.20
  127.1 10.1 %collective-permute-done.25.band_mine = bf16[128,2048]{1,0:T(8,128)(2,1)S(1)} collective-permute-done((bf16[128,2048]{1,0:T(8,128)(2,1)}, bf16[128,2048]{1,0:T(8,128)(2,1)S(1)}, u32[]{:S(2)}, u32[]{:S(2)}) %collective-permute-start.25) | collective-permute-done | bytes 524320 | tf_op jit(solution)/shard_map/ppermute | solution.py:34
  137.1 0.7 collective-permute-start.21
  137.8 6.1 %collective-permute-start.32 = (bf16[128,2048]{1,0:T(8,128)(2,1)S(1)}, bf16[128,2048]{1,0:T(8,128)(2,1)S(1)}, u32[]{:S(2)}, u32[]{:S(2)}) collective-permute-start(bf16[128,2048]{1,0:T(8,128)(2,1)S(1)} %copy-done.2), channel_id=1, source_target_pairs={{192,224},{193,225},{194,226},{195,227},{196,228},{197,229},{198,2... | collective-permute-start | bytes 1572872 | tf_op jit(solution)/shard_map/ppermute | solution.py:34
  143.9 6.8 %collective-permute-done.24 = bf16[32,2048]{1,0:T(8,128)(2,1)S(1)} collective-permute-done((bf16[32,2048]{1,0:T(8,128)(2,1)S(1)}, bf16[32,2048]{1,0:T(8,128)(2,1)S(1)}, u32[]{:S(2)}, u32[]{:S(2)}) %collective-permute-start.24) | collective-permute-done | bytes 131104 | tf_op jit(solution)/shard_map/ppermute | solution.py:34
  150.7 0.4 fusion.2
  151.1 0.3 fusion.8
  151.4 0.3 fusion.6
  151.7 0.7 collective-permute-start.22
  152.4 0.2 collective-permute-done.26.band_other
  152.6 1.4 shard_map.58
  154.0 1.3 collective-permute-start.31
  155.3 1.3 collective-permute-start.27
  156.6 1.3 collective-permute-start.28
  157.9 1.3 collective-permute-start.29
  159.2 4.0 %collective-permute-done.32.band_mine = bf16[128,2048]{1,0:T(8,128)(2,1)S(1)} collective-permute-done((bf16[128,2048]{1,0:T(8,128)(2,1)S(1)}, bf16[128,2048]{1,0:T(8,128)(2,1)S(1)}, u32[]{:S(2)}, u32[]{:S(2)}) %collective-permute-start.32) | collective-permute-done | bytes 524320 | tf_op jit(solution)/shard_map/ppermute | solution.py:34
  163.2 1.3 collective-permute-start.30
  164.5 10.8 %collective-permute-done.31 = bf16[32,2048]{1,0:T(8,128)(2,1)S(1)} collective-permute-done((bf16[32,2048]{1,0:T(8,128)(2,1)S(1)}, bf16[32,2048]{1,0:T(8,128)(2,1)S(1)}, u32[]{:S(2)}, u32[]{:S(2)}) %collective-permute-start.31) | collective-permute-done | bytes 131104 | tf_op jit(solution)/shard_map/ppermute | solution.py:34
  175.3 0.4 fusion
  175.7 0.3 fusion.12
  176.1 0.3 fusion.13
  176.4 1.8 collective-permute-done.27.q0
  178.1 5.5 %collective-permute-done.28.q1 = bf16[32,2048]{1,0:T(8,128)(2,1)S(1)} collective-permute-done((bf16[32,2048]{1,0:T(8,128)(2,1)S(1)}, bf16[32,2048]{1,0:T(8,128)(2,1)S(1)}, u32[]{:S(2)}, u32[]{:S(2)}) %collective-permute-start.28) | collective-permute-done | bytes 131104 | tf_op jit(solution)/shard_map/ppermute | solution.py:34
  183.7 1.6 collective-permute-done.29.q2
  185.4 1.9 shard_map.59
  187.3 18.1 %all_to_all.10 = bf16[8,32,256]{2,1,0:T(8,128)(2,1)S(1)} all-to-all(bf16[8,32,256]{2,1,0:T(8,128)(2,1)S(1)} %bitcast.25), channel_id=1, replica_groups=mesh['x'=4,'zh'=2,'y'=4,'zl'=4,'core'=2] {'zh','y'}, dimensions={0} | all-to-all | bytes 262144 | tf_op jit(solution)/shard_map/all_to_all | solution.py:217
  205.4 0.6 bitcast_reduce_fusion
  (57 shorter events, 0.5 us)
Async XLA Ops:
  0.0 33.2 %copy-start.3 = (bf16[3072,64]{0,1:T(8,128)(2,1)S(1)}, bf16[3072,64]{0,1:T(8,128)(2,1)}, u32[]{:S(2)}) copy-start(bf16[3072,64]{0,1:T(8,128)(2,1)} %param.6) | copy-start | bytes 1179652
  0.0 33.2 %collective-permute-start.2 = (bf16[64,3072]{1,0:T(8,128)(2,1)}, bf16[64,3072]{1,0:T(8,128)(2,1)S(1)}, u32[]{:S(2)}, u32[]{:S(2)}) collective-permute-start(bf16[64,3072]{1,0:T(8,128)(2,1)} %bitcast.26), channel_id=1, source_target_pairs={{0,2},{2,4},{4,6},{6,0},{1,3},{3,5},{5,7},{7,1},{8,10},{10,12},{12... | collective-permute-start | bytes 1179656 | tf_op jit(solution)/shard_map/ppermute | solution.py:135
  0.0 36.6 %collective-permute-start.4 = (bf16[64,3072]{1,0:T(8,128)(2,1)}, bf16[64,3072]{1,0:T(8,128)(2,1)S(1)}, u32[]{:S(2)}, u32[]{:S(2)}) collective-permute-start(bf16[64,3072]{1,0:T(8,128)(2,1)} %bitcast.27), channel_id=1, source_target_pairs={{0,4},{2,6},{4,0},{6,2},{1,5},{3,7},{5,1},{7,3},{8,12},{10,14},{12... | collective-permute-start | bytes 1179656 | tf_op jit(solution)/shard_map/ppermute | solution.py:135
  1.6 35.0 %collective-permute-start.6 = (bf16[64,3072]{1,0:T(8,128)(2,1)}, bf16[64,3072]{1,0:T(8,128)(2,1)S(1)}, u32[]{:S(2)}, u32[]{:S(2)}) collective-permute-start(bf16[64,3072]{1,0:T(8,128)(2,1)} %bitcast.28), channel_id=1, source_target_pairs={{0,6},{2,0},{4,2},{6,4},{1,7},{3,1},{5,3},{7,5},{8,14},{10,8},{12,... | collective-permute-start | bytes 1179656 | tf_op jit(solution)/shard_map/ppermute | solution.py:135
  2.8 30.4 %collective-permute-start = (bf16[32,256]{1,0:T(8,128)(2,1)S(1)}, bf16[32,256]{1,0:T(8,128)(2,1)S(1)}, u32[]{:S(2)}, u32[]{:S(2)}) collective-permute-start(bf16[32,256]{1,0:T(8,128)(2,1)S(1)} %broadcast_select_fusion), channel_id=1, source_target_pairs={{0,32},{32,0},{1,33},{33,1},{2,34},{34,2},{3,35},{35,3},{4,36},{36... | collective-permute-start | bytes 49160 | tf_op jit(solution)/shard_map/ppermute | solution.py:131
  33.2 3.9 %collective-permute-start.1 = (bf16[64,3072]{1,0:T(8,128)(2,1)S(1)}, bf16[64,3072]{1,0:T(8,128)(2,1)S(1)}, u32[]{:S(2)}, u32[]{:S(2)}) collective-permute-start(bf16[64,3072]{1,0:T(8,128)(2,1)S(1)} %bitcast.30), channel_id=1, source_target_pairs={{0,1},{1,0},{2,3},{3,2},{4,5},{5,4},{6,7},{7,6},{8,9},{9,8},{10,11... | collective-permute-start | bytes 1179656 | tf_op jit(solution)/shard_map/ppermute | solution.py:38
  33.2 5.7 %copy-start.4 = (bf16[64,3072]{1,0:T(8,128)(2,1)}, bf16[64,3072]{1,0:T(8,128)(2,1)S(1)}, u32[]{:S(2)}) copy-start(bf16[64,3072]{1,0:T(8,128)(2,1)S(1)} %collective-permute-done.2.refs_2_) | copy-start | bytes 1179652
  33.2 3.9 %collective-permute-start.3 = (bf16[64,3072]{1,0:T(8,128)(2,1)S(1)}, bf16[64,3072]{1,0:T(8,128)(2,1)S(1)}, u32[]{:S(2)}, u32[]{:S(2)}) collective-permute-start(bf16[64,3072]{1,0:T(8,128)(2,1)S(1)} %collective-permute-done.2.refs_2_), channel_id=1, source_target_pairs={{0,1},{1,0},{2,3},{3,2},{4,5},{5,4},{6,7},{7,6},{8,9},{9,8},{10,11... | collective-permute-start | bytes 1179656 | tf_op jit(solution)/shard_map/ppermute | solution.py:38
  36.6 2.3 %copy-start.5 = (bf16[64,3072]{1,0:T(8,128)(2,1)}, bf16[64,3072]{1,0:T(8,128)(2,1)S(1)}, u32[]{:S(2)}) copy-start(bf16[64,3072]{1,0:T(8,128)(2,1)S(1)} %collective-permute-done.4.refs_4_) | copy-start | bytes 1179652
  36.6 1.7 collective-permute-start.5
  36.6 2.3 %copy-start.6 = (bf16[64,3072]{1,0:T(8,128)(2,1)}, bf16[64,3072]{1,0:T(8,128)(2,1)S(1)}, u32[]{:S(2)}) copy-start(bf16[64,3072]{1,0:T(8,128)(2,1)S(1)} %collective-permute-done.6.refs_6_) | copy-start | bytes 1179652
  36.6 2.3 %collective-permute-start.7 = (bf16[64,3072]{1,0:T(8,128)(2,1)S(1)}, bf16[64,3072]{1,0:T(8,128)(2,1)S(1)}, u32[]{:S(2)}, u32[]{:S(2)}) collective-permute-start(bf16[64,3072]{1,0:T(8,128)(2,1)S(1)} %collective-permute-done.6.refs_6_), channel_id=1, source_target_pairs={{0,1},{1,0},{2,3},{3,2},{4,5},{5,4},{6,7},{7,6},{8,9},{9,8},{10,11... | collective-permute-start | bytes 1179656 | tf_op jit(solution)/shard_map/ppermute | solution.py:38
  37.1 1.8 copy-start.7
  37.1 1.8 copy-start.8
  38.3 0.7 copy-start.9
  39.1 0.7 copy-start.10
  47.7 68.8 %copy-start.11 = (bf16[256,64]{0,1:T(8,128)(2,1)S(1)}, bf16[256,64]{0,1:T(8,128)(2,1)}, u32[]{:S(2)}) copy-start(bf16[256,64]{0,1:T(8,128)(2,1)} %param.9) | copy-start | bytes 98308
  47.7 68.9 %copy-start.1 = (bf16[2048,256]{1,0:T(8,128)(2,1)S(1)}, bf16[2048,256]{1,0:T(8,128)(2,1)}, u32[]{:S(2)}) copy-start(bf16[2048,256]{1,0:T(8,128)(2,1)} %inverse.7) | copy-start | bytes 3145732
  47.7 23.2 %all-to-all-start = ((bf16[16,128,256]{2,1,0:T(8,128)(2,1)}), bf16[16,128,256]{2,1,0:T(8,128)(2,1)S(1)}, u32[]{:S(2)}, u32[]{:S(2)}) async-start(bf16[16,128,256]{2,1,0:T(8,128)(2,1)} %bitcast.24), calls=%async_computation | async-start | bytes 2097152 | tf_op jit(solution)/shard_map/all_to_all | solution.py:144
  55.3 19.4 %collective-permute-start.8 = (bf16[1024,256]{1,0:T(8,128)(2,1)S(1)}, bf16[1024,256]{1,0:T(8,128)(2,1)S(1)}, u32[]{:S(2)}, u32[]{:S(2)}) collective-permute-start(bf16[1024,256]{1,0:T(8,128)(2,1)S(1)} %constant_dynamic-slice_fusion.1), channel_id=1, source_target_pairs={{0,32},{1,33},{2,34},{3,35},{4,36},{5,37},{6,38},{7,39},{8,40},{9,... | collective-permute-start | bytes 1572872 | tf_op jit(solution)/shard_map/ppermute | solution.py:34
  74.8 1.3 collective-permute-start.9
  76.1 16.2 %collective-permute-start.10 = (f32[32,512]{1,0:T(8,128)S(1)}, f32[32,512]{1,0:T(8,128)S(1)}, u32[]{:S(2)}, u32[]{:S(2)}) collective-permute-start(f32[32,512]{1,0:T(8,128)S(1)} %get-tuple-element.75), channel_id=1, source_target_pairs={{0,0},{1,1},{2,66},{3,67},{4,132},{5,133},{6,198},{7,199},{8,8},{9... | collective-permute-start | bytes 196616 | tf_op jit(solution)/shard_map/ppermute | solution.py:34
  78.1 16.2 %collective-permute-start.11 = (f32[32,512]{1,0:T(8,128)S(1)}, f32[32,512]{1,0:T(8,128)S(1)}, u32[]{:S(2)}, u32[]{:S(2)}) collective-permute-start(f32[32,512]{1,0:T(8,128)S(1)} %get-tuple-element.74), channel_id=1, source_target_pairs={{0,32},{1,33},{2,98},{3,99},{4,164},{5,165},{6,230},{7,231},{8,40}... | collective-permute-start | bytes 196616 | tf_op jit(solution)/shard_map/ppermute | solution.py:34
  94.3 19.1 %collective-permute-start.17 = (bf16[128,2048]{1,0:T(8,128)(2,1)}, bf16[128,2048]{1,0:T(8,128)(2,1)S(1)}, u32[]{:S(2)}, u32[]{:S(2)}) collective-permute-start(bf16[128,2048]{1,0:T(8,128)(2,1)} %get-tuple-element.57), channel_id=1, source_target_pairs={{64,96},{65,97},{66,98},{67,99},{68,100},{69,101},{70,102},{71,103... | collective-permute-start | bytes 1572872 | tf_op jit(solution)/shard_map/ppermute | solution.py:34
  96.5 20.1 %collective-permute-start.12 = (bf16[1024,256]{1,0:T(8,128)(2,1)S(1)}, bf16[1024,256]{1,0:T(8,128)(2,1)S(1)}, u32[]{:S(2)}, u32[]{:S(2)}) collective-permute-start(bf16[1024,256]{1,0:T(8,128)(2,1)S(1)} %collective-permute-done.8.far_mine), channel_id=1, source_target_pairs={{0,1},{1,0},{2,3},{3,2},{4,5},{5,4},{6,7},{7,6},{8,9},{9,8},{10,11... | collective-permute-start | bytes 1572872 | tf_op jit(solution)/shard_map/ppermute | solution.py:38
  113.4 6.7 %collective-permute-start.18 = (bf16[128,2048]{1,0:T(8,128)(2,1)S(1)}, bf16[128,2048]{1,0:T(8,128)(2,1)S(1)}, u32[]{:S(2)}, u32[]{:S(2)}) collective-permute-start(bf16[128,2048]{1,0:T(8,128)(2,1)S(1)} %collective-permute-done.17.band_mine), channel_id=1, source_target_pairs={{0,1},{1,0},{2,3},{3,2},{4,5},{5,4},{6,7},{7,6},{8,9},{9,8},{10,11... | collective-permute-start | bytes 1572872 | tf_op jit(solution)/shard_map/ppermute | solution.py:38
  113.4 23.7 %collective-permute-start.25 = (bf16[128,2048]{1,0:T(8,128)(2,1)}, bf16[128,2048]{1,0:T(8,128)(2,1)S(1)}, u32[]{:S(2)}, u32[]{:S(2)}) collective-permute-start(bf16[128,2048]{1,0:T(8,128)(2,1)} %get-tuple-element.63), channel_id=1, source_target_pairs={{128,160},{129,161},{130,162},{131,163},{132,164},{133,165},{134,1... | collective-permute-start | bytes 1572872 | tf_op jit(solution)/shard_map/ppermute | solution.py:34
  116.6 21.2 %copy-start.2 = (bf16[128,2048]{1,0:T(8,128)(2,1)S(1)}, bf16[128,2048]{1,0:T(8,128)(2,1)}, u32[]{:S(2)}) copy-start(bf16[128,2048]{1,0:T(8,128)(2,1)} %get-tuple-element.69) | copy-start | bytes 1572868
  117.4 2.0 collective-permute-start.13
  118.1 2.0 collective-permute-start.14
  118.7 1.4 collective-permute-start.15
  119.4 0.7 collective-permute-start.16
  120.1 2.2 %copy-start = (bf16[256,8192]{1,0:T(8,128)(2,1)S(1)}, bf16[256,8192]{1,0:T(8,128)(2,1)}, u32[]{:S(2)}) copy-start(bf16[256,8192]{1,0:T(8,128)(2,1)} %band.5) | copy-start | bytes 12582916
  123.7 14.1 %collective-permute-start.23 = (bf16[32,2048]{1,0:T(8,128)(2,1)S(1)}, bf16[32,2048]{1,0:T(8,128)(2,1)S(1)}, u32[]{:S(2)}, u32[]{:S(2)}) collective-permute-start(bf16[32,2048]{1,0:T(8,128)(2,1)S(1)} %get-tuple-element.60), channel_id=1, source_target_pairs={{64,128},{65,129},{66,130},{67,131},{68,132},{69,133},{70,134},{71... | collective-permute-start | bytes 393224 | tf_op jit(solution)/shard_map/ppermute | solution.py:34
  124.4 26.3 %collective-permute-start.24 = (bf16[32,2048]{1,0:T(8,128)(2,1)S(1)}, bf16[32,2048]{1,0:T(8,128)(2,1)S(1)}, u32[]{:S(2)}, u32[]{:S(2)}) collective-permute-start(bf16[32,2048]{1,0:T(8,128)(2,1)S(1)} %get-tuple-element.60), channel_id=1, source_target_pairs={{64,192},{65,193},{66,194},{67,195},{68,196},{69,197},{70,198},{71... | collective-permute-start | bytes 393224 | tf_op jit(solution)/shard_map/ppermute | solution.py:34
  125.7 26.0 %collective-permute-start.19 = (bf16[32,2048]{1,0:T(8,128)(2,1)S(1)}, bf16[32,2048]{1,0:T(8,128)(2,1)S(1)}, u32[]{:S(2)}, u32[]{:S(2)}) collective-permute-start(bf16[32,2048]{1,0:T(8,128)(2,1)S(1)} %get-tuple-element.58), channel_id=1, source_target_pairs={{64,128},{65,129},{66,130},{67,131},{68,132},{69,133},{70,134},{71... | collective-permute-start | bytes 393224 | tf_op jit(solution)/shard_map/ppermute | solution.py:34
  126.4 26.0 %collective-permute-start.20 = (bf16[32,2048]{1,0:T(8,128)(2,1)S(1)}, bf16[32,2048]{1,0:T(8,128)(2,1)S(1)}, u32[]{:S(2)}, u32[]{:S(2)}) collective-permute-start(bf16[32,2048]{1,0:T(8,128)(2,1)S(1)} %get-tuple-element.58), channel_id=1, source_target_pairs={{64,136},{65,137},{66,138},{67,139},{68,140},{69,141},{70,142},{71... | collective-permute-start | bytes 393224 | tf_op jit(solution)/shard_map/ppermute | solution.py:34
  137.1 15.3 %collective-permute-start.21 = (bf16[32,2048]{1,0:T(8,128)(2,1)S(1)}, bf16[32,2048]{1,0:T(8,128)(2,1)S(1)}, u32[]{:S(2)}, u32[]{:S(2)}) collective-permute-start(bf16[32,2048]{1,0:T(8,128)(2,1)S(1)} %get-tuple-element.58), channel_id=1, source_target_pairs={{64,144},{65,145},{66,146},{67,147},{68,148},{69,149},{70,150},{71... | collective-permute-start | bytes 393224 | tf_op jit(solution)/shard_map/ppermute | solution.py:34
  137.8 25.4 %collective-permute-start.32 = (bf16[128,2048]{1,0:T(8,128)(2,1)S(1)}, bf16[128,2048]{1,0:T(8,128)(2,1)S(1)}, u32[]{:S(2)}, u32[]{:S(2)}) collective-permute-start(bf16[128,2048]{1,0:T(8,128)(2,1)S(1)} %copy-done.2), channel_id=1, source_target_pairs={{192,224},{193,225},{194,226},{195,227},{196,228},{197,229},{198,2... | collective-permute-start | bytes 1572872 | tf_op jit(solution)/shard_map/ppermute | solution.py:34
  150.7 1.9 collective-permute-start.26
  151.7 0.7 collective-permute-start.22
  154.0 21.4 %collective-permute-start.31 = (bf16[32,2048]{1,0:T(8,128)(2,1)S(1)}, bf16[32,2048]{1,0:T(8,128)(2,1)S(1)}, u32[]{:S(2)}, u32[]{:S(2)}) collective-permute-start(bf16[32,2048]{1,0:T(8,128)(2,1)S(1)} %get-tuple-element.66), channel_id=1, source_target_pairs={{128,192},{129,193},{130,194},{131,195},{132,196},{133,197},{134,1... | collective-permute-start | bytes 393224 | tf_op jit(solution)/shard_map/ppermute | solution.py:34
  155.3 22.9 %collective-permute-start.27 = (bf16[32,2048]{1,0:T(8,128)(2,1)S(1)}, bf16[32,2048]{1,0:T(8,128)(2,1)S(1)}, u32[]{:S(2)}, u32[]{:S(2)}) collective-permute-start(bf16[32,2048]{1,0:T(8,128)(2,1)S(1)} %get-tuple-element.64), channel_id=1, source_target_pairs={{128,192},{129,193},{130,194},{131,195},{132,196},{133,197},{134,1... | collective-permute-start | bytes 393224 | tf_op jit(solution)/shard_map/ppermute | solution.py:34
  156.6 27.1 %collective-permute-start.28 = (bf16[32,2048]{1,0:T(8,128)(2,1)S(1)}, bf16[32,2048]{1,0:T(8,128)(2,1)S(1)}, u32[]{:S(2)}, u32[]{:S(2)}) collective-permute-start(bf16[32,2048]{1,0:T(8,128)(2,1)S(1)} %get-tuple-element.64), channel_id=1, source_target_pairs={{128,200},{129,201},{130,202},{131,203},{132,204},{133,205},{134,2... | collective-permute-start | bytes 393224 | tf_op jit(solution)/shard_map/ppermute | solution.py:34
  157.9 27.4 %collective-permute-start.29 = (bf16[32,2048]{1,0:T(8,128)(2,1)S(1)}, bf16[32,2048]{1,0:T(8,128)(2,1)S(1)}, u32[]{:S(2)}, u32[]{:S(2)}) collective-permute-start(bf16[32,2048]{1,0:T(8,128)(2,1)S(1)} %get-tuple-element.64), channel_id=1, source_target_pairs={{128,208},{129,209},{130,210},{131,211},{132,212},{133,213},{134,2... | collective-permute-start | bytes 393224 | tf_op jit(solution)/shard_map/ppermute | solution.py:34
  163.2 22.2 %collective-permute-start.30 = (bf16[32,2048]{1,0:T(8,128)(2,1)S(1)}, bf16[32,2048]{1,0:T(8,128)(2,1)S(1)}, u32[]{:S(2)}, u32[]{:S(2)}) collective-permute-start(bf16[32,2048]{1,0:T(8,128)(2,1)S(1)} %get-tuple-element.64), channel_id=1, source_target_pairs={{128,216},{129,217},{130,218},{131,219},{132,220},{133,221},{134,2... | collective-permute-start | bytes 393224 | tf_op jit(solution)/shard_map/ppermute | solution.py:34
  175.3 10.0 %collective-permute-start.33 = (bf16[128,2048]{1,0:T(8,128)(2,1)S(1)}, bf16[128,2048]{1,0:T(8,128)(2,1)S(1)}, u32[]{:S(2)}, u32[]{:S(2)}) collective-permute-start(bf16[128,2048]{1,0:T(8,128)(2,1)S(1)} %collective-permute-done.32.band_mine), channel_id=1, source_target_pairs={{0,1},{1,0},{2,3},{3,2},{4,5},{5,4},{6,7},{7,6},{8,9},{9,8},{10,11... | collective-permute-start | bytes 1572872 | tf_op jit(solution)/shard_map/ppermute | solution.py:38

commit v3 on v2

--- a/solution.py
+++ b/solution.py
@@ -40,6 +40,10 @@
 
 def other_half(first_plane):
     return lambda x, zh, y, zl, core: (x, 1 - zh, y, zl, core) if x >= first_plane else None
+
+
+def mirrored(x, zh, y, zl, core):
+    return x, 1 - zh, y, 3 - zl, core
 
 
 def by_core(core, mine, other):
@@ -125,6 +129,8 @@
         lax.dynamic_slice(band, (core * (rows // 2), k * nb), (rows // 2, nb)) for k in range(STEPS - 1)
     ]
     half_inverse = lax.dynamic_slice_in_dim(inv_diag, core * (nb // 2), nb // 2, 0)
+    far_inverse = permute(half_inverse, mirrored)
+    blocks = [band[:, k * nb : (k + 1) * nb] for k in range(STEPS - 1)]
     source = rhs.T
     sent_half = jnp.where(zh == 0, source[half:], source[:half])
     mine_half = jnp.where(zh == 0, source[:half], source[half:])
@@ -134,27 +140,29 @@
     parts = [
         lax.ppermute(mine, "zl", [(i, (i + d) % 4) for i in range(4)]) for d in (1, 2, 3)
     ]
-    mine, slices, half_inverse, far_source = lax.optimization_barrier((mine, slices, half_inverse, far_source))
+    mine, slices, blocks, far_source = lax.optimization_barrier((mine, slices, blocks, far_source))
     pairs = [q for p in [mine] + parts for q in (p, swap_core(p))]
-    pairs, half_inverse = lax.optimization_barrier((pairs, half_inverse))
-    far_inverse = permute(half_inverse, other_half(0))
+    far_inverse2 = swap_core(far_inverse)
+    pairs, far_inverse, far_inverse2, slices = lax.optimization_barrier((pairs, far_inverse, far_inverse2, slices))
 
     partial = partial_products(pairs, old_factor, rows)
     partial = partial.reshape(16, 2 * own_columns, rows)
+    far_band = permute(slices[0], other_half(1))
     summed = lax.all_to_all(partial, ("x", "y"), 0, 0, tiled=True).astype(F32).sum(0)
-    summed, far_inverse = lax.optimization_barrier((summed, far_inverse))
-    far_inverse2 = swap_core(far_inverse)
-    other = swap_core(summed[own_columns:])
-    both = by_core(core, summed[:own_columns], other)
-    stay = jnp.where(zh == 0, both[:half], both[half:])
-    leave = jnp.where(zh == 0, both[half:], both[:half])
-    stay = permute(stay, lambda x, zh, y, zl, core: (zl, zh, y, (zl - x) % 4, core))
-    leave = permute(leave, lambda x, zh, y, zl, core: (zl, 1 - zh, y, (zl - x) % 4, core))
-    stay, leave, slices = lax.optimization_barrier((stay, leave, slices))
-    earlier = stay + leave
-
-    near = mine_half.astype(F32) - jnp.where(zh == 0, earlier[:, :rows], earlier[:, rows:])
-    far = far_source.astype(F32) - jnp.where(zh == 0, earlier[:, rows:], earlier[:, :rows])
+    halves = []
+    for e in range(2):
+        tile = summed[e * own_columns : (e + 1) * own_columns]
+        stay = jnp.where(zh == 0, tile[:half], tile[half:])
+        leave = jnp.where(zh == 0, tile[half:], tile[:half])
+        halves.append((
+            permute(stay, lambda x, zh, y, zl, core, e=e: (zl, zh, y, (zl - x) % 4, core ^ e)),
+            permute(leave, lambda x, zh, y, zl, core, e=e: (zl, 1 - zh, y, (zl - x) % 4, core ^ e)),
+        ))
+    halves, slices, far_band = lax.optimization_barrier((halves, slices, far_band))
+    same, cross = halves[0][0] + halves[0][1], halves[1][0] + halves[1][1]
+
+    near = mine_half.astype(F32) - jnp.where(core == zh, same, cross)
+    far = far_source.astype(F32) - jnp.where(core == zh, cross, same)
 
     params = pltpu.CompilerParams(vmem_limit_bytes=24 * 2**20)
     whole_shape = jax.ShapeDtypeStruct((half, nb), BF16)
@@ -168,14 +176,7 @@
         compiler_params=params,
     )(core_arr, near, far, inv_diag, far_inverse, far_inverse2)
     passed = []
-    far_band = None
     for k in range(STEPS - 1):
-        following = slices[k]
-        if far_band is not None:
-            following, _ = lax.optimization_barrier((following, far_band))
-        before = far_band
-        far_band = permute(following, other_half(k + 1))
-        far_band2 = swap_core(far_band)
         pieces = [
             permute(
                 term,
@@ -183,17 +184,18 @@
             )
             for d in range(4)
         ]
+        if k > 0:
+            before, before2 = far_band, far_band2
+            far_band = permute(following, other_half(k + 1))
+            far_band, pieces = lax.optimization_barrier((far_band, pieces))
+        far_band2 = swap_core(far_band)
         if passed:
             late = sum(passed)
-            near = near - mul_t(late, band[:, (k - 1) * nb : k * nb])
+            near = near - mul_t(late, blocks[k - 1])
             far = far - by_core(core, mul_t(late, before), mul_t(late, before2))
         near, far, whole, term = pl.pallas_call(
             step_kernel,
-            grid=(1,),
-            in_specs=[SMEM]
-            + [VMEM] * 6
-            + [pl.BlockSpec((rows, nb), lambda i, k=k: (0, k))]
-            + [VMEM] * 5,
+            in_specs=[SMEM] + [VMEM] * 12,
             out_specs=[VMEM] * 4,
             out_shape=[
                 jax.ShapeDtypeStruct(near.shape, F32),
@@ -203,8 +205,9 @@
             ],
             scratch_shapes=scratch,
             compiler_params=params,
-        )(core_arr, *pieces, near, far, band, far_band, far_band2, inv_diag, far_inverse, far_inverse2)
-        before2 = far_band2
+        )(core_arr, *pieces, near, far, blocks[k], far_band, far_band2, inv_diag, far_inverse, far_inverse2)
+        if k + 2 < STEPS:
+            following, whole = lax.optimization_barrier((slices[k + 1], whole))
         passed = [
             permute(
                 whole,

time: 209 us -> 199 us (0.952); the launches traced: 206 us -> 198 us
  waiting for transfers between devices: 100 us -> 82.8 us
  starting transfers between devices: 63.6 us -> 57.4 us
  local copies, waits for them, and re-layouts: 6.77 us -> 12.8 us
  matrix products: 1.93 us -> 6.36 us
  Pallas kernels: 13.3 us -> 15.7 us
    ppermute x21 -> x23, waiting for transfers between devices: 63 us -> 53 us  [permute(): return lax.ppermute(array, AXES, moves(target))]
    ppermute x21 -> x23, starting transfers between devices: 46.9 us -> 38.6 us  [permute(): return lax.ppermute(array, AXES, moves(target))]
    ppermute x1, waiting for transfers between devices: 20.8 us -> 13.2 us  [body(): far_source = lax.ppermute(sent_half, 'zh', [(0, 1), (1, 0)])]
    dot_general x6, matrix products: 1.93 us -> 6.36 us  [mul_t(): lax.dot_general(left, right, (((1,), (1,)), ((), ())), preferred_element_...]
    all_to_all x1, waiting for transfers between devices: 10.3 us -> 13.9 us  [body(): lax.all_to_all(partial, ('x', 'y'), 0, 0, tiled=True).astype(F32).sum(0)]
    slice x1, local copies, waits for them, and re-layouts: 0.01 us -> 3.28 us  [body(): blocks = [band[:, k * nb:(k + 1) * nb] for k in range(STEPS - 1)]]
    ppermute x3, waiting for transfers between devices: 2.9 us -> 0.01 us  [body(): lax.ppermute(mine, 'zl', [(i, (i + d) % 4) for i in range(4)])]
    unnamed x24 -> x32, local copies, waits for them, and re-layouts: 3.11 us -> 5.72 us
  transfers between devices with their start and end apart: 35 -> 36, of which waited for: 18 -> 17; matrix products, arithmetic and copies ran while one was open for 3% -> 8% of each run, Pallas kernels for 2% -> 0%
where the time goes in v3:
time: 199 us; the launch traced here: 198 us
  waiting for transfers between devices  82.8 us (42%)
  starting transfers between devices  57.4 us (29%)
  blocking collectives  19.1 us (10%)
  Pallas kernels  15.7 us (8%)
  local copies, waits for them, and re-layouts  12.8 us (6%)
  matrix products  6.36 us (3%)
  other arithmetic  3.62 us (2%)
    ppermute x23, waiting for transfers between devices, permute(): return lax.ppermute(array, AXES, moves(target))  53 us
    ppermute x23, starting transfers between devices, permute(): return lax.ppermute(array, AXES, moves(target))  38.6 us
    all_to_all x1, blocking collectives, body(): term = lax.all_to_all(term, ('zh', 'y'), 0, 0, tiled=True)  19.1 us
    all_to_all x1, waiting for transfers between devices, body(): lax.all_to_all(partial, ('x', 'y'), 0, 0, tiled=True).astype(F32).sum(0)  13.9 us
    ppermute x1, waiting for transfers between devices, body(): far_source = lax.ppermute(sent_half, 'zh', [(0, 1), (1, 0)])  13.2 us
    pallas_call x1, Pallas kernels, partial_products(): pl.pallas_call(partial_kernel, grid=(groups,), in_specs=[pl.BlockSpec((wi...  7.94 us
    all_to_all x1, starting transfers between devices, body(): lax.all_to_all(partial, ('x', 'y'), 0, 0, tiled=True).astype(F32).sum(0)  7.55 us
    pallas_call x3, Pallas kernels, body(): pl.pallas_call(step_kernel, in_specs=[SMEM] + [VMEM] * 12, out_specs=[VME...  7.03 us
  transfers between devices with their start and end apart: 36, of which 17 were waited for; matrix products, arithmetic and copies ran while one was open for 8% of the time, Pallas kernels for 0%

profile of v3, /device:TPU:102, one launch (start us, length us, event | category | flops | bytes accessed | tf_op | source)
XLA Modules:
  0.0 198.2 jit_solution(7069019417415367190)
XLA Ops:
  0.0 1.6 collective-permute-start.4
  2.0 0.7 broadcast_select_fusion
  2.8 5.9 %collective-permute-start = (bf16[32,256]{1,0:T(8,128)(2,1)S(1)}, bf16[32,256]{1,0:T(8,128)(2,1)}, u32[]{:S(2)}, u32[]{:S(2)}) collective-permute-start(bf16[32,256]{1,0:T(8,128)(2,1)S(1)} %broadcast_select_fusion), channel_id=1, source_target_pairs={{0,32},{32,0},{1,33},{33,1},{2,34},{34,2},{3,35},{35,3},{4,36},{36... | collective-permute-start | bytes 49160 | tf_op jit(solution)/shard_map/ppermute | solution.py:137
  8.7 1.1 constant_dynamic-slice_fusion.1
  10.0 3.3 %fusion.8 = (bf16[256,2048]{1,0:T(8,128)(2,1)}, bf16[256,2048]{1,0:T(8,128)(2,1)S(1)}, bf16[256,2048]{1,0:T(8,128)(2,1)S(1)}) fusion(bf16[256,8192]{1,0:T(8,128)(2,1)} %param.7), kind=kLoop, calls=%fused_computation.24 | loop fusion | bytes 6291456 | tf_op jit(solution)/shard_map/slice | solution.py:133
  13.3 15.2 %collective-permute-done.8.far_mine = bf16[1024,256]{1,0:T(8,128)(2,1)S(1)} collective-permute-done((bf16[1024,256]{1,0:T(8,128)(2,1)S(1)}, bf16[1024,256]{1,0:T(8,128)(2,1)S(1)}, u32[]{:S(2)}, u32[]{:S(2)}) %collective-permute-start.8) | collective-permute-done | bytes 524320 | tf_op jit(solution)/shard_map/ppermute | solution.py:34
  28.5 2.7 %constant_dynamic-slice_fusion = (bf16[128,2048]{1,0:T(8,128)(2,1)}, bf16[128,2048]{1,0:T(8,128)(2,1)}, bf16[128,2048]{1,0:T(8,128)(2,1)}) fusion(bf16[256,8192]{1,0:T(8,128)(2,1)} %param.7, s32[]{:T(128)S(6)} %select_n.59), kind=kLoop, calls=%fused_computation.14 | loop fusion | bytes 3145732 | tf_op jit(solution)/shard_map/dynamic_slice | solution.py:129
  31.3 13.2 %collective-permute-done = bf16[32,256]{1,0:T(8,128)(2,1)} collective-permute-done((bf16[32,256]{1,0:T(8,128)(2,1)S(1)}, bf16[32,256]{1,0:T(8,128)(2,1)}, u32[]{:S(2)}, u32[]{:S(2)}) %collective-permute-start) | collective-permute-done | bytes 16416 | tf_op jit(solution)/shard_map/ppermute | solution.py:137
  45.5 0.7 collective-permute-done.1.refs_1_
  46.1 0.8 collective-permute-done.3.refs_3_
  46.9 0.6 collective-permute-done.5.refs_5_
  47.5 0.6 collective-permute-done.7.refs_7_
  48.2 0.6 copy-done.15
  48.8 0.8 copy-done.5
  49.6 7.9 %shard_map.55 = bf16[4,4,128,256]{3,2,1,0:T(8,128)(2,1)} custom-call(bf16[64,3072]{1,0:T(8,128)(2,1)} %bitcast.31, bf16[64,3072]{1,0:T(8,128)(2,1)} %copy-done.12, bf16[64,3072]{1,0:T(8,128)(2,1)} %collective-permute-done.2.refs_2_, bf16[64,3072]{1,0:T(8,128)(2,1)} %copy-done.13, bf16[64,3072]{1,0:T(8,128)(2,1)} %collective-permute-done.4.refs_4_, ...), custom_call_target="tpu_custom_call" | custom-call | tf_op jit(solution)/shard_map/pallas_call | solution.py:72
  57.5 7.5 %all-to-all-start = ((bf16[16,128,256]{2,1,0:T(8,128)(2,1)}), bf16[16,128,256]{2,1,0:T(8,128)(2,1)}, u32[]{:S(2)}, u32[]{:S(2)}) async-start(bf16[16,128,256]{2,1,0:T(8,128)(2,1)} %bitcast.26), calls=%async_computation | async-start | bytes 2097152 | tf_op jit(solution)/shard_map/all_to_all | solution.py:151
  65.1 1.9 collective-permute-start.14
  67.0 13.9 %all-to-all-done = bf16[16,128,256]{2,1,0:T(8,128)(2,1)} async-done(((bf16[16,128,256]{2,1,0:T(8,128)(2,1)}), bf16[16,128,256]{2,1,0:T(8,128)(2,1)}, u32[]{:S(2)}, u32[]{:S(2)}) %all-to-all-start) | async-done | bytes 1048608 | tf_op jit(solution)/shard_map/all_to_all | solution.py:151
  80.9 1.4 convert_reduce_fusion
  82.3 1.9 collective-permute-start.10
  84.2 4.6 %collective-permute-start.11 = (f32[32,256]{1,0:T(8,128)S(1)}, f32[32,256]{1,0:T(8,128)S(1)}, u32[]{:S(2)}, u32[]{:S(2)}) collective-permute-start(f32[32,256]{1,0:T(8,128)S(1)} %get-tuple-element.118), channel_id=1, source_target_pairs={{0,32},{1,33},{2,98},{3,99},{4,164},{5,165},{6,230},{7,231},{8,40}... | collective-permute-start | bytes 98312 | tf_op jit(solution)/shard_map/ppermute | solution.py:34
  88.8 2.9 %collective-permute-start.13 = (f32[32,256]{1,0:T(8,128)S(1)}, f32[32,256]{1,0:T(8,128)S(1)}, u32[]{:S(2)}, u32[]{:S(2)}) collective-permute-start(f32[32,256]{1,0:T(8,128)S(1)} %get-tuple-element.115), channel_id=1, source_target_pairs={{0,33},{1,32},{2,99},{3,98},{4,165},{5,164},{6,231},{7,230},{8,41}... | collective-permute-start | bytes 98312 | tf_op jit(solution)/shard_map/ppermute | solution.py:34
  91.7 6.5 %collective-permute-done.14.band_mine = bf16[128,2048]{1,0:T(8,128)(2,1)} collective-permute-done((bf16[128,2048]{1,0:T(8,128)(2,1)}, bf16[128,2048]{1,0:T(8,128)(2,1)}, u32[]{:S(2)}, u32[]{:S(2)}) %collective-permute-start.14) | collective-permute-done | bytes 524320 | tf_op jit(solution)/shard_map/ppermute | solution.py:34
  98.3 2.2 %collective-permute-start.19 = (bf16[128,2048]{1,0:T(8,128)(2,1)}, bf16[128,2048]{1,0:T(8,128)(2,1)}, u32[]{:S(2)}, u32[]{:S(2)}) collective-permute-start(bf16[128,2048]{1,0:T(8,128)(2,1)} %collective-permute-done.14.band_mine), channel_id=1, source_target_pairs={{0,1},{1,0},{2,3},{3,2},{4,5},{5,4},{6,7},{7,6},{8,9},{9,8},{10,11... | collective-permute-start | bytes 1572872 | tf_op jit(solution)/shard_map/ppermute | solution.py:38
  100.5 0.8 select_subtract_fusion
  101.3 1.0 copy-done.2
  102.3 1.0 copy-done.6
  103.4 0.7 shard_map.56
  104.1 0.7 collective-permute-start.15
  104.8 0.7 collective-permute-start.16
  105.4 0.7 collective-permute-start.17
  106.1 0.8 collective-permute-start.18
  107.0 2.6 %shard_map.57 = (f32[32,256]{1,0:T(8,128)S(1)}, f32[32,256]{1,0:T(8,128)S(1)}, bf16[32,2048]{1,0:T(8,128)(2,1)S(1)}, bf16[32,2048]{1,0:T(8,128)(2,1)S(1)}) custom-call(s32[1]{0:T(128)} %bitcast.core_ref, bf16[32,2048]{1,0:T(8,128)(2,1)S(1)} %collective-permute-done.15.q0, bf16[32,2048]{1,0:T(8,128)(2,1)S(1)} %collective-permute-done.16.q1, ...), custom_call_target="tpu_custom_call" | custom-call | tf_op jit(solution)/shard_map/pallas_call | solution.py:196
  109.6 6.0 %collective-permute-start.20 = (bf16[128,2048]{1,0:T(8,128)(2,1)}, bf16[128,2048]{1,0:T(8,128)(2,1)}, u32[]{:S(2)}, u32[]{:S(2)}) collective-permute-start(bf16[128,2048]{1,0:T(8,128)(2,1)} %get-tuple-element.83), channel_id=1, source_target_pairs={{128,160},{129,161},{130,162},{131,163},{132,164},{133,165},{134,1... | collective-permute-start | bytes 1572872 | tf_op jit(solution)/shard_map/ppermute | solution.py:34
  115.6 1.3 collective-permute-start.25
  116.9 1.3 collective-permute-start.26
  118.2 0.8 collective-permute-start.21
  119.0 0.7 collective-permute-start.22
  119.7 0.7 collective-permute-start.23
  120.4 11.3 %collective-permute-done.26 = bf16[32,2048]{1,0:T(8,128)(2,1)} collective-permute-done((bf16[32,2048]{1,0:T(8,128)(2,1)S(1)}, bf16[32,2048]{1,0:T(8,128)(2,1)}, u32[]{:S(2)}, u32[]{:S(2)}) %collective-permute-start.26) | collective-permute-done | bytes 131104 | tf_op jit(solution)/shard_map/ppermute | solution.py:34
  131.7 0.7 collective-permute-start.24
  132.4 1.4 fusion.6
  133.8 6.0 %collective-permute-done.20.band_mine = bf16[128,2048]{1,0:T(8,128)(2,1)} collective-permute-done((bf16[128,2048]{1,0:T(8,128)(2,1)}, bf16[128,2048]{1,0:T(8,128)(2,1)}, u32[]{:S(2)}, u32[]{:S(2)}) %collective-permute-start.20) | collective-permute-done | bytes 524320 | tf_op jit(solution)/shard_map/ppermute | solution.py:34
  139.9 1.5 fusion.4
  141.4 1.5 fusion.2
  143.0 1.0 copy-done.3
  144.0 1.0 copy-done.7
  145.0 2.5 %shard_map.58 = (f32[32,256]{1,0:T(8,128)S(1)}, f32[32,256]{1,0:T(8,128)S(1)}, bf16[32,2048]{1,0:T(8,128)(2,1)S(1)}, bf16[32,2048]{1,0:T(8,128)(2,1)S(1)}) custom-call(s32[1]{0:T(128)} %bitcast.core_ref, bf16[32,2048]{1,0:T(8,128)(2,1)S(1)} %collective-permute-done.21.q0, bf16[32,2048]{1,0:T(8,128)(2,1)S(1)} %collective-permute-done.22.q1, ...), custom_call_target="tpu_custom_call" | custom-call | tf_op jit(solution)/shard_map/pallas_call | solution.py:196
  147.6 6.4 %collective-permute-start.28 = (bf16[128,2048]{1,0:T(8,128)(2,1)S(1)}, bf16[128,2048]{1,0:T(8,128)(2,1)S(1)}, u32[]{:S(2)}, u32[]{:S(2)}) collective-permute-start(bf16[128,2048]{1,0:T(8,128)(2,1)S(1)} %copy-done.10), channel_id=1, source_target_pairs={{192,224},{193,225},{194,226},{195,227},{196,228},{197,229},{198,2... | collective-permute-start | bytes 1572872 | tf_op jit(solution)/shard_map/ppermute | solution.py:34
  154.0 1.3 collective-permute-start.33
  155.3 1.3 collective-permute-start.29
  156.6 1.3 collective-permute-start.30
  157.9 1.3 collective-permute-start.31
  159.2 3.0 %collective-permute-done.33 = bf16[32,2048]{1,0:T(8,128)(2,1)S(1)} collective-permute-done((bf16[32,2048]{1,0:T(8,128)(2,1)S(1)}, bf16[32,2048]{1,0:T(8,128)(2,1)S(1)}, u32[]{:S(2)}, u32[]{:S(2)}) %collective-permute-start.33) | collective-permute-done | bytes 131104 | tf_op jit(solution)/shard_map/ppermute | solution.py:34
  162.2 1.3 collective-permute-start.32
  163.9 1.1 collective-permute-done.29.q0
  165.0 3.5 %collective-permute-done.30.q1 = bf16[32,2048]{1,0:T(8,128)(2,1)S(1)} collective-permute-done((bf16[32,2048]{1,0:T(8,128)(2,1)S(1)}, bf16[32,2048]{1,0:T(8,128)(2,1)S(1)}, u32[]{:S(2)}, u32[]{:S(2)}) %collective-permute-start.30) | collective-permute-done | bytes 131104 | tf_op jit(solution)/shard_map/ppermute | solution.py:34
  168.5 3.4 %collective-permute-done.31.q2 = bf16[32,2048]{1,0:T(8,128)(2,1)S(1)} collective-permute-done((bf16[32,2048]{1,0:T(8,128)(2,1)S(1)}, bf16[32,2048]{1,0:T(8,128)(2,1)S(1)}, u32[]{:S(2)}, u32[]{:S(2)}) %collective-permute-start.31) | collective-permute-done | bytes 131104 | tf_op jit(solution)/shard_map/ppermute | solution.py:34
  171.9 1.3 collective-permute-done.32.q3
  173.2 1.4 collective-permute-done.28.band_mine
  174.7 1.3 fusion.10
  176.6 1.9 shard_map.59
  178.5 19.1 %all_to_all.10 = bf16[8,32,256]{2,1,0:T(8,128)(2,1)S(1)} all-to-all(bf16[8,32,256]{2,1,0:T(8,128)(2,1)S(1)} %bitcast.27), channel_id=1, replica_groups=mesh['x'=4,'zh'=2,'y'=4,'zl'=4,'core'=2] {'zh','y'}, dimensions={0} | all-to-all | bytes 262144 | tf_op jit(solution)/shard_map/all_to_all | solution.py:220
  197.6 0.6 bitcast_reduce_fusion
  (65 shorter events, 3.0 us)
Async XLA Ops:
  0.0 44.4 %collective-permute-start.2 = (bf16[64,3072]{1,0:T(8,128)(2,1)}, bf16[64,3072]{1,0:T(8,128)(2,1)}, u32[]{:S(2)}, u32[]{:S(2)}) collective-permute-start(bf16[64,3072]{1,0:T(8,128)(2,1)} %bitcast.28), channel_id=1, source_target_pairs={{0,2},{2,4},{4,6},{6,0},{1,3},{3,5},{5,7},{7,1},{8,10},{10,12},{12... | collective-permute-start | bytes 1179656 | tf_op jit(solution)/shard_map/ppermute | solution.py:141
  0.0 44.9 %collective-permute-start.4 = (bf16[64,3072]{1,0:T(8,128)(2,1)}, bf16[64,3072]{1,0:T(8,128)(2,1)}, u32[]{:S(2)}, u32[]{:S(2)}) collective-permute-start(bf16[64,3072]{1,0:T(8,128)(2,1)} %bitcast.29), channel_id=1, source_target_pairs={{0,4},{2,6},{4,0},{6,2},{1,5},{3,7},{5,1},{7,3},{8,12},{10,14},{12... | collective-permute-start | bytes 1179656 | tf_op jit(solution)/shard_map/ppermute | solution.py:141
  1.6 43.5 %collective-permute-start.6 = (bf16[64,3072]{1,0:T(8,128)(2,1)}, bf16[64,3072]{1,0:T(8,128)(2,1)}, u32[]{:S(2)}, u32[]{:S(2)}) collective-permute-start(bf16[64,3072]{1,0:T(8,128)(2,1)} %bitcast.30), channel_id=1, source_target_pairs={{0,6},{2,0},{4,2},{6,4},{1,7},{3,1},{5,3},{7,5},{8,14},{10,8},{12,... | collective-permute-start | bytes 1179656 | tf_op jit(solution)/shard_map/ppermute | solution.py:141
  2.8 41.6 %collective-permute-start = (bf16[32,256]{1,0:T(8,128)(2,1)S(1)}, bf16[32,256]{1,0:T(8,128)(2,1)}, u32[]{:S(2)}, u32[]{:S(2)}) collective-permute-start(bf16[32,256]{1,0:T(8,128)(2,1)S(1)} %broadcast_select_fusion), channel_id=1, source_target_pairs={{0,32},{32,0},{1,33},{33,1},{2,34},{34,2},{3,35},{35,3},{4,36},{36... | collective-permute-start | bytes 49160 | tf_op jit(solution)/shard_map/ppermute | solution.py:137
  9.8 34.6 %copy-start.11 = (bf16[3072,64]{0,1:T(8,128)(2,1)S(1)}, bf16[3072,64]{0,1:T(8,128)(2,1)}, u32[]{:S(2)}) copy-start(bf16[3072,64]{0,1:T(8,128)(2,1)} %param.6) | copy-start | bytes 1179652
  9.8 18.7 %collective-permute-start.8 = (bf16[1024,256]{1,0:T(8,128)(2,1)S(1)}, bf16[1024,256]{1,0:T(8,128)(2,1)S(1)}, u32[]{:S(2)}, u32[]{:S(2)}) collective-permute-start(bf16[1024,256]{1,0:T(8,128)(2,1)S(1)} %constant_dynamic-slice_fusion.1), channel_id=1, source_target_pairs={{0,38},{1,39},{2,36},{3,37},{4,34},{5,35},{6,32},{7,33},{8,46},{9,... | collective-permute-start | bytes 1572872 | tf_op jit(solution)/shard_map/ppermute | solution.py:34
  28.5 19.5 %copy-start.1 = (bf16[1024,256]{1,0:T(8,128)(2,1)}, bf16[1024,256]{1,0:T(8,128)(2,1)S(1)}, u32[]{:S(2)}) copy-start(bf16[1024,256]{1,0:T(8,128)(2,1)S(1)} %collective-permute-done.8.far_mine) | copy-start | bytes 1572868
  28.5 19.5 %collective-permute-start.9 = (bf16[1024,256]{1,0:T(8,128)(2,1)S(1)}, bf16[1024,256]{1,0:T(8,128)(2,1)S(1)}, u32[]{:S(2)}, u32[]{:S(2)}) collective-permute-start(bf16[1024,256]{1,0:T(8,128)(2,1)S(1)} %collective-permute-done.8.far_mine), channel_id=1, source_target_pairs={{0,1},{1,0},{2,3},{3,2},{4,5},{5,4},{6,7},{7,6},{8,9},{9,8},{10,11... | collective-permute-start | bytes 1572872 | tf_op jit(solution)/shard_map/ppermute | solution.py:38
  44.4 1.7 collective-permute-start.1
  44.4 2.5 %collective-permute-start.3 = (bf16[64,3072]{1,0:T(8,128)(2,1)}, bf16[64,3072]{1,0:T(8,128)(2,1)S(1)}, u32[]{:S(2)}, u32[]{:S(2)}) collective-permute-start(bf16[64,3072]{1,0:T(8,128)(2,1)} %collective-permute-done.2.refs_2_), channel_id=1, source_target_pairs={{0,1},{1,0},{2,3},{3,2},{4,5},{5,4},{6,7},{7,6},{8,9},{9,8},{10,11... | collective-permute-start | bytes 1179656 | tf_op jit(solution)/shard_map/ppermute | solution.py:38
  44.9 2.5 %collective-permute-start.5 = (bf16[64,3072]{1,0:T(8,128)(2,1)}, bf16[64,3072]{1,0:T(8,128)(2,1)S(1)}, u32[]{:S(2)}, u32[]{:S(2)}) collective-permute-start(bf16[64,3072]{1,0:T(8,128)(2,1)} %collective-permute-done.4.refs_4_), channel_id=1, source_target_pairs={{0,1},{1,0},{2,3},{3,2},{4,5},{5,4},{6,7},{7,6},{8,9},{9,8},{10,11... | collective-permute-start | bytes 1179656 | tf_op jit(solution)/shard_map/ppermute | solution.py:38
  45.0 3.0 %collective-permute-start.7 = (bf16[64,3072]{1,0:T(8,128)(2,1)}, bf16[64,3072]{1,0:T(8,128)(2,1)S(1)}, u32[]{:S(2)}, u32[]{:S(2)}) collective-permute-start(bf16[64,3072]{1,0:T(8,128)(2,1)} %collective-permute-done.6.refs_6_), channel_id=1, source_target_pairs={{0,1},{1,0},{2,3},{3,2},{4,5},{5,4},{6,7},{7,6},{8,9},{9,8},{10,11... | collective-permute-start | bytes 1179656 | tf_op jit(solution)/shard_map/ppermute | solution.py:38
  46.1 1.9 copy-start.12
  46.9 1.1 copy-start.13
  47.5 0.8 copy-start.14
  48.0 0.8 copy-start.15
  48.8 0.8 copy-start.5
  57.5 43.7 %copy-start = (bf16[2048,256]{1,0:T(8,128)(2,1)S(1)}, bf16[2048,256]{1,0:T(8,128)(2,1)}, u32[]{:S(2)}) copy-start(bf16[2048,256]{1,0:T(8,128)(2,1)} %inverse.7) | copy-start | bytes 3145732
  57.5 23.3 %all-to-all-start = ((bf16[16,128,256]{2,1,0:T(8,128)(2,1)}), bf16[16,128,256]{2,1,0:T(8,128)(2,1)}, u32[]{:S(2)}, u32[]{:S(2)}) async-start(bf16[16,128,256]{2,1,0:T(8,128)(2,1)} %bitcast.26), calls=%async_computation | async-start | bytes 2097152 | tf_op jit(solution)/shard_map/all_to_all | solution.py:151
  65.1 33.1 %collective-permute-start.14 = (bf16[128,2048]{1,0:T(8,128)(2,1)}, bf16[128,2048]{1,0:T(8,128)(2,1)}, u32[]{:S(2)}, u32[]{:S(2)}) collective-permute-start(bf16[128,2048]{1,0:T(8,128)(2,1)} %get-tuple-element.68), channel_id=1, source_target_pairs={{64,96},{65,97},{66,98},{67,99},{68,100},{69,101},{70,102},{71,103... | collective-permute-start | bytes 1572872 | tf_op jit(solution)/shard_map/ppermute | solution.py:34
  82.3 16.0 %collective-permute-start.10 = (f32[32,256]{1,0:T(8,128)S(1)}, f32[32,256]{1,0:T(8,128)S(1)}, u32[]{:S(2)}, u32[]{:S(2)}) collective-permute-start(f32[32,256]{1,0:T(8,128)S(1)} %get-tuple-element.117), channel_id=1, source_target_pairs={{0,0},{1,1},{2,66},{3,67},{4,132},{5,133},{6,198},{7,199},{8,8},{9... | collective-permute-start | bytes 98312 | tf_op jit(solution)/shard_map/ppermute | solution.py:34
  84.2 14.0 %collective-permute-start.11 = (f32[32,256]{1,0:T(8,128)S(1)}, f32[32,256]{1,0:T(8,128)S(1)}, u32[]{:S(2)}, u32[]{:S(2)}) collective-permute-start(f32[32,256]{1,0:T(8,128)S(1)} %get-tuple-element.118), channel_id=1, source_target_pairs={{0,32},{1,33},{2,98},{3,99},{4,164},{5,165},{6,230},{7,231},{8,40}... | collective-permute-start | bytes 98312 | tf_op jit(solution)/shard_map/ppermute | solution.py:34
  88.8 9.5 %collective-permute-start.12 = (f32[32,256]{1,0:T(8,128)S(1)}, f32[32,256]{1,0:T(8,128)S(1)}, u32[]{:S(2)}, u32[]{:S(2)}) collective-permute-start(f32[32,256]{1,0:T(8,128)S(1)} %get-tuple-element.116), channel_id=1, source_target_pairs={{0,1},{1,0},{2,67},{3,66},{4,133},{5,132},{6,199},{7,198},{8,9},{9... | collective-permute-start | bytes 98312 | tf_op jit(solution)/shard_map/ppermute | solution.py:34
  88.8 9.5 %collective-permute-start.13 = (f32[32,256]{1,0:T(8,128)S(1)}, f32[32,256]{1,0:T(8,128)S(1)}, u32[]{:S(2)}, u32[]{:S(2)}) collective-permute-start(f32[32,256]{1,0:T(8,128)S(1)} %get-tuple-element.115), channel_id=1, source_target_pairs={{0,33},{1,32},{2,99},{3,98},{4,165},{5,164},{6,231},{7,230},{8,41}... | collective-permute-start | bytes 98312 | tf_op jit(solution)/shard_map/ppermute | solution.py:34
  98.3 8.8 %collective-permute-start.19 = (bf16[128,2048]{1,0:T(8,128)(2,1)}, bf16[128,2048]{1,0:T(8,128)(2,1)}, u32[]{:S(2)}, u32[]{:S(2)}) collective-permute-start(bf16[128,2048]{1,0:T(8,128)(2,1)} %collective-permute-done.14.band_mine), channel_id=1, source_target_pairs={{0,1},{1,0},{2,3},{3,2},{4,5},{5,4},{6,7},{7,6},{8,9},{9,8},{10,11... | collective-permute-start | bytes 1572872 | tf_op jit(solution)/shard_map/ppermute | solution.py:38
  101.3 1.0 copy-start.2
  102.3 1.0 copy-start.6
  104.1 2.9 %collective-permute-start.15 = (bf16[32,2048]{1,0:T(8,128)(2,1)S(1)}, bf16[32,2048]{1,0:T(8,128)(2,1)S(1)}, u32[]{:S(2)}, u32[]{:S(2)}) collective-permute-start(bf16[32,2048]{1,0:T(8,128)(2,1)S(1)} %shard_map.56), channel_id=1, source_target_pairs={{0,64},{1,65},{2,66},{3,67},{4,68},{5,69},{6,70},{7,71},{8,72},{9,... | collective-permute-start | bytes 393224 | tf_op jit(solution)/shard_map/ppermute | solution.py:34
  104.8 2.2 %collective-permute-start.16 = (bf16[32,2048]{1,0:T(8,128)(2,1)S(1)}, bf16[32,2048]{1,0:T(8,128)(2,1)S(1)}, u32[]{:S(2)}, u32[]{:S(2)}) collective-permute-start(bf16[32,2048]{1,0:T(8,128)(2,1)S(1)} %shard_map.56), channel_id=1, source_target_pairs={{0,72},{1,73},{2,74},{3,75},{4,76},{5,77},{6,78},{7,79},{8,80},{9,... | collective-permute-start | bytes 393224 | tf_op jit(solution)/shard_map/ppermute | solution.py:34
  105.4 1.6 collective-permute-start.17
  106.1 0.9 collective-permute-start.18
  109.6 30.2 %collective-permute-start.20 = (bf16[128,2048]{1,0:T(8,128)(2,1)}, bf16[128,2048]{1,0:T(8,128)(2,1)}, u32[]{:S(2)}, u32[]{:S(2)}) collective-permute-start(bf16[128,2048]{1,0:T(8,128)(2,1)} %get-tuple-element.83), channel_id=1, source_target_pairs={{128,160},{129,161},{130,162},{131,163},{132,164},{133,165},{134,1... | collective-permute-start | bytes 1572872 | tf_op jit(solution)/shard_map/ppermute | solution.py:34
  115.6 4.1 %collective-permute-start.25 = (bf16[32,2048]{1,0:T(8,128)(2,1)S(1)}, bf16[32,2048]{1,0:T(8,128)(2,1)}, u32[]{:S(2)}, u32[]{:S(2)}) collective-permute-start(bf16[32,2048]{1,0:T(8,128)(2,1)S(1)} %get-tuple-element.90), channel_id=1, source_target_pairs={{64,128},{65,129},{66,130},{67,131},{68,132},{69,133},{70,134},{71... | collective-permute-start | bytes 393224 | tf_op jit(solution)/shard_map/ppermute | solution.py:34
  116.9 14.8 %collective-permute-start.26 = (bf16[32,2048]{1,0:T(8,128)(2,1)S(1)}, bf16[32,2048]{1,0:T(8,128)(2,1)}, u32[]{:S(2)}, u32[]{:S(2)}) collective-permute-start(bf16[32,2048]{1,0:T(8,128)(2,1)S(1)} %get-tuple-element.90), channel_id=1, source_target_pairs={{64,192},{65,193},{66,194},{67,195},{68,196},{69,197},{70,198},{71... | collective-permute-start | bytes 393224 | tf_op jit(solution)/shard_map/ppermute | solution.py:34
  118.2 29.4 %copy-start.10 = (bf16[128,2048]{1,0:T(8,128)(2,1)S(1)}, bf16[128,2048]{1,0:T(8,128)(2,1)}, u32[]{:S(2)}) copy-start(bf16[128,2048]{1,0:T(8,128)(2,1)} %get-tuple-element.95) | copy-start | bytes 1572868
  118.2 15.6 %collective-permute-start.21 = (bf16[32,2048]{1,0:T(8,128)(2,1)S(1)}, bf16[32,2048]{1,0:T(8,128)(2,1)S(1)}, u32[]{:S(2)}, u32[]{:S(2)}) collective-permute-start(bf16[32,2048]{1,0:T(8,128)(2,1)S(1)} %get-tuple-element.84), channel_id=1, source_target_pairs={{64,128},{65,129},{66,130},{67,131},{68,132},{69,133},{70,134},{71... | collective-permute-start | bytes 393224 | tf_op jit(solution)/shard_map/ppermute | solution.py:34
  119.0 14.8 %collective-permute-start.22 = (bf16[32,2048]{1,0:T(8,128)(2,1)S(1)}, bf16[32,2048]{1,0:T(8,128)(2,1)S(1)}, u32[]{:S(2)}, u32[]{:S(2)}) collective-permute-start(bf16[32,2048]{1,0:T(8,128)(2,1)S(1)} %get-tuple-element.84), channel_id=1, source_target_pairs={{64,136},{65,137},{66,138},{67,139},{68,140},{69,141},{70,142},{71... | collective-permute-start | bytes 393224 | tf_op jit(solution)/shard_map/ppermute | solution.py:34
  119.7 14.1 %collective-permute-start.23 = (bf16[32,2048]{1,0:T(8,128)(2,1)S(1)}, bf16[32,2048]{1,0:T(8,128)(2,1)S(1)}, u32[]{:S(2)}, u32[]{:S(2)}) collective-permute-start(bf16[32,2048]{1,0:T(8,128)(2,1)S(1)} %get-tuple-element.84), channel_id=1, source_target_pairs={{64,144},{65,145},{66,146},{67,147},{68,148},{69,149},{70,150},{71... | collective-permute-start | bytes 393224 | tf_op jit(solution)/shard_map/ppermute | solution.py:34
  131.7 2.1 %collective-permute-start.24 = (bf16[32,2048]{1,0:T(8,128)(2,1)S(1)}, bf16[32,2048]{1,0:T(8,128)(2,1)S(1)}, u32[]{:S(2)}, u32[]{:S(2)}) collective-permute-start(bf16[32,2048]{1,0:T(8,128)(2,1)S(1)} %get-tuple-element.84), channel_id=1, source_target_pairs={{64,152},{65,153},{66,154},{67,155},{68,156},{69,157},{70,158},{71... | collective-permute-start | bytes 393224 | tf_op jit(solution)/shard_map/ppermute | solution.py:34
  139.9 3.1 %collective-permute-start.27 = (bf16[128,2048]{1,0:T(8,128)(2,1)}, bf16[128,2048]{1,0:T(8,128)(2,1)S(1)}, u32[]{:S(2)}, u32[]{:S(2)}) collective-permute-start(bf16[128,2048]{1,0:T(8,128)(2,1)} %collective-permute-done.20.band_mine), channel_id=1, source_target_pairs={{0,1},{1,0},{2,3},{3,2},{4,5},{5,4},{6,7},{7,6},{8,9},{9,8},{10,11... | collective-permute-start | bytes 1572872 | tf_op jit(solution)/shard_map/ppermute | solution.py:38
  139.9 36.7 %copy-start.8 = (bf16[1024,256]{1,0:T(8,128)(2,1)S(1)}, bf16[1024,256]{1,0:T(8,128)(2,1)}, u32[]{:S(2)}) copy-start(bf16[1024,256]{1,0:T(8,128)(2,1)} %copy-done.5) | copy-start | bytes 1572868
  141.4 35.2 %copy-start.4 = (bf16[1024,256]{1,0:T(8,128)(2,1)S(1)}, bf16[1024,256]{1,0:T(8,128)(2,1)}, u32[]{:S(2)}) copy-start(bf16[1024,256]{1,0:T(8,128)(2,1)} %copy-done.1) | copy-start | bytes 1572868
  143.0 1.0 copy-start.3
  144.0 1.0 copy-start.7
  145.0 31.5 %copy-start.9 = (bf16[256,2048]{1,0:T(8,128)(2,1)S(1)}, bf16[256,2048]{1,0:T(8,128)(2,1)}, u32[]{:S(2)}) copy-start(bf16[256,2048]{1,0:T(8,128)(2,1)} %get-tuple-element.104.band) | copy-start | bytes 3145732
  147.6 27.1 %collective-permute-start.28 = (bf16[128,2048]{1,0:T(8,128)(2,1)S(1)}, bf16[128,2048]{1,0:T(8,128)(2,1)S(1)}, u32[]{:S(2)}, u32[]{:S(2)}) collective-permute-start(bf16[128,2048]{1,0:T(8,128)(2,1)S(1)} %copy-done.10), channel_id=1, source_target_pairs={{192,224},{193,225},{194,226},{195,227},{196,228},{197,229},{198,2... | collective-permute-start | bytes 1572872 | tf_op jit(solution)/shard_map/ppermute | solution.py:34
  154.0 8.2 %collective-permute-start.33 = (bf16[32,2048]{1,0:T(8,128)(2,1)S(1)}, bf16[32,2048]{1,0:T(8,128)(2,1)S(1)}, u32[]{:S(2)}, u32[]{:S(2)}) collective-permute-start(bf16[32,2048]{1,0:T(8,128)(2,1)S(1)} %get-tuple-element.102), channel_id=1, source_target_pairs={{128,192},{129,193},{130,194},{131,195},{132,196},{133,197},{134,1... | collective-permute-start | bytes 393224 | tf_op jit(solution)/shard_map/ppermute | solution.py:34
  155.3 9.7 %collective-permute-start.29 = (bf16[32,2048]{1,0:T(8,128)(2,1)S(1)}, bf16[32,2048]{1,0:T(8,128)(2,1)S(1)}, u32[]{:S(2)}, u32[]{:S(2)}) collective-permute-start(bf16[32,2048]{1,0:T(8,128)(2,1)S(1)} %get-tuple-element.96), channel_id=1, source_target_pairs={{128,192},{129,193},{130,194},{131,195},{132,196},{133,197},{134,1... | collective-permute-start | bytes 393224 | tf_op jit(solution)/shard_map/ppermute | solution.py:34
  156.6 12.0 %collective-permute-start.30 = (bf16[32,2048]{1,0:T(8,128)(2,1)S(1)}, bf16[32,2048]{1,0:T(8,128)(2,1)S(1)}, u32[]{:S(2)}, u32[]{:S(2)}) collective-permute-start(bf16[32,2048]{1,0:T(8,128)(2,1)S(1)} %get-tuple-element.96), channel_id=1, source_target_pairs={{128,200},{129,201},{130,202},{131,203},{132,204},{133,205},{134,2... | collective-permute-start | bytes 393224 | tf_op jit(solution)/shard_map/ppermute | solution.py:34
  157.9 14.1 %collective-permute-start.31 = (bf16[32,2048]{1,0:T(8,128)(2,1)S(1)}, bf16[32,2048]{1,0:T(8,128)(2,1)S(1)}, u32[]{:S(2)}, u32[]{:S(2)}) collective-permute-start(bf16[32,2048]{1,0:T(8,128)(2,1)S(1)} %get-tuple-element.96), channel_id=1, source_target_pairs={{128,208},{129,209},{130,210},{131,211},{132,212},{133,213},{134,2... | collective-permute-start | bytes 393224 | tf_op jit(solution)/shard_map/ppermute | solution.py:34
  162.2 11.0 %collective-permute-start.32 = (bf16[32,2048]{1,0:T(8,128)(2,1)S(1)}, bf16[32,2048]{1,0:T(8,128)(2,1)S(1)}, u32[]{:S(2)}, u32[]{:S(2)}) collective-permute-start(bf16[32,2048]{1,0:T(8,128)(2,1)S(1)} %get-tuple-element.96), channel_id=1, source_target_pairs={{128,216},{129,217},{130,218},{131,219},{132,220},{133,221},{134,2... | collective-permute-start | bytes 393224 | tf_op jit(solution)/shard_map/ppermute | solution.py:34
  174.7 1.9 collective-permute-start.34

commit v4 on v3

--- a/solution.py
+++ b/solution.py
@@ -1,3 +1,5 @@
+import functools
+
 import jax
 import jax.numpy as jnp
 from jax import lax
@@ -44,6 +46,10 @@
 
 def mirrored(x, zh, y, zl, core):
     return x, 1 - zh, y, 3 - zl, core
+
+
+def mirrored_from(first_plane):
+    return lambda x, *rest: mirrored(x, *rest) if x >= first_plane else None
 
 
 def by_core(core, mine, other):
@@ -95,20 +101,32 @@
     term_of(core_ref[0], near[...], far[...], inverse, far_mine, far_other, out, total)
 
 
-def step_kernel(
-    core_ref, q0, q1, q2, q3, near, far, band, band_mine, band_other, inverse, far_mine, far_other,
-    near_out, far_out, whole, out, total,
-):
+def step_kernel(late_count, core_ref, *refs):
+    near, far, inverse, far_mine, far_other = refs[:5]
+    pieces, updates, refs = refs[5:9], [refs[9:12]], refs[12:]
     core = core_ref[0]
-    size = band_mine.shape[0]
-    newest = q0[...].astype(F32) + q1[...].astype(F32) + q2[...].astype(F32) + q3[...].astype(F32)
-    newest = newest.astype(BF16)
-    whole[...] = newest
-    near_out[...] = near[...] - mul_t(newest, band[...])
+    newest = sum(q[...].astype(F32) for q in pieces).astype(BF16)
+    width = newest.shape[1]
+    known = [newest]
+    late = None
+    if late_count:
+        late, refs = refs[0], refs[1:]
+        for i in range(late_count):
+            known.append(late[:, i * width : (i + 1) * width])
+            updates.append(refs[:3])
+            refs = refs[3:]
+    near_out, far_out, whole, out, total = refs
+    if late_count:
+        whole[:, : late_count * width] = late[...]
+    whole[:, late_count * width :] = newest
+    near_out[...] = near[...]
     far_out[...] = far[...]
-    for at, part in ((core, band_mine), (1 - core, band_other)):
-        place = pl.ds(pl.multiple_of(at * size, size), size)
-        far_out[:, place] -= mul_t(newest, part[...])
+    for value, (rows, mine, other) in zip(known, updates):
+        near_out[...] -= mul_t(value, rows[...])
+        size = mine.shape[0]
+        for at, part in ((core, mine), (1 - core, other)):
+            place = pl.ds(pl.multiple_of(at * size, size), size)
+            far_out[:, place] -= mul_t(value, part[...])
     term_of(core, near_out[...], far_out[...], inverse, far_mine, far_other, out, total)
 
 
@@ -147,7 +165,7 @@
 
     partial = partial_products(pairs, old_factor, rows)
     partial = partial.reshape(16, 2 * own_columns, rows)
-    far_band = permute(slices[0], other_half(1))
+    far_band = permute(slices[0], mirrored_from(1))
     summed = lax.all_to_all(partial, ("x", "y"), 0, 0, tiled=True).astype(F32).sum(0)
     halves = []
     for e in range(2):
@@ -175,46 +193,47 @@
         scratch_shapes=scratch,
         compiler_params=params,
     )(core_arr, near, far, inv_diag, far_inverse, far_inverse2)
-    passed = []
+
+    def to_next(term, k, d):
+        return permute(
+            term, lambda x, zh, y, zl, core: (x + 1, zh, (y + d) % 4, zl, core) if x == k else None
+        )
+
+    late, known_bands = None, []
+    following, term = lax.optimization_barrier((slices[1], term))
+    next_band = permute(following, other_half(2))
     for k in range(STEPS - 1):
-        pieces = [
-            permute(
-                term,
-                lambda x, zh, y, zl, core, d=d: (x + 1, zh, (y + d) % 4, zl, core) if x == k else None,
-            )
-            for d in range(4)
-        ]
+        pieces = [to_next(term, k, d) for d in (1, 2, 3)]
         if k > 0:
-            before, before2 = far_band, far_band2
-            far_band = permute(following, other_half(k + 1))
-            far_band, pieces = lax.optimization_barrier((far_band, pieces))
-        far_band2 = swap_core(far_band)
-        if passed:
-            late = sum(passed)
-            near = near - mul_t(late, blocks[k - 1])
-            far = far - by_core(core, mul_t(late, before), mul_t(late, before2))
+            term, late = lax.optimization_barrier((term, late))
+        pieces.append(to_next(term, k, 0))
+        far_band, pieces = lax.optimization_barrier((far_band, pieces))
+        bands = (blocks[k], far_band, swap_core(far_band))
+        operands = [*pieces, *bands]
+        if k > 0:
+            operands += [late, *[a for old in known_bands for a in old]]
+        known_bands.append(bands)
+        if k == 1:
+            following, _ = lax.optimization_barrier((slices[2], far_band))
+            next_band = permute(following, other_half(3))
         near, far, whole, term = pl.pallas_call(
-            step_kernel,
-            in_specs=[SMEM] + [VMEM] * 12,
+            functools.partial(step_kernel, k),
+            in_specs=[SMEM] + [VMEM] * (5 + len(operands)),
             out_specs=[VMEM] * 4,
             out_shape=[
                 jax.ShapeDtypeStruct(near.shape, F32),
                 jax.ShapeDtypeStruct(far.shape, F32),
-                whole_shape,
+                jax.ShapeDtypeStruct((half, (k + 1) * nb), BF16),
                 whole_shape,
             ],
             scratch_shapes=scratch,
             compiler_params=params,
-        )(core_arr, *pieces, near, far, blocks[k], far_band, far_band2, inv_diag, far_inverse, far_inverse2)
+        )(core_arr, near, far, inv_diag, far_inverse, far_inverse2, *operands)
         if k + 2 < STEPS:
-            following, whole = lax.optimization_barrier((slices[k + 1], whole))
-        passed = [
-            permute(
-                whole,
-                lambda x, zh, y, zl, core, hop=hop: (k + hop, zh, y, zl, core) if x == k + 1 else None,
+            late = permute(
+                whole, lambda x, zh, y, zl, core: (x + 1, zh, y, zl, core) if x == k + 1 else None
             )
-            for hop in range(2, STEPS - k)
-        ]
+            far_band = next_band
 
     term = term.reshape(half, 8, rows).transpose(1, 0, 2)
     term = lax.all_to_all(term, ("zh", "y"), 0, 0, tiled=True)

time: 199 us -> 192 us (0.965)
  matrix products: 6.36 us -> 0 us
  waiting for transfers between devices: 82.8 us -> 86.4 us
  blocking collectives: 19.1 us -> 16.4 us
  Pallas kernels: 15.7 us -> 18.4 us
  local copies, waits for them, and re-layouts: 12.8 us -> 10.6 us
  starting transfers between devices: 57.4 us -> 55.4 us
    ppermute x23 -> x22, waiting for transfers between devices: 53 us -> 61.1 us  [permute(): return lax.ppermute(array, AXES, moves(target))]
    dot_general x6 -> x0, matrix products: 6.36 us -> none  [mul_t(): lax.dot_general(left, right, (((1,), (1,)), ((), ())), preferred_element_...]
    ppermute x1, waiting for transfers between devices: 13.2 us -> 6.92 us  [body(): far_source = lax.ppermute(sent_half, 'zh', [(0, 1), (1, 0)])]
    pallas_call x3, Pallas kernels: 7.03 us -> 9.78 us  [body(): pl.pallas_call(functools.partial(step_kernel, k), in_specs=[SMEM] + [VMEM...]
    all_to_all x1, blocking collectives: 19.1 us -> 16.4 us  [body(): term = lax.all_to_all(term, ('zh', 'y'), 0, 0, tiled=True)]
    unnamed x32 -> x24, local copies, waits for them, and re-layouts: 5.72 us -> 3.63 us
    ppermute x8, starting transfers between devices: 3.27 us -> 1.23 us  [swap_core(): return lax.ppermute(array, 'core', [(0, 1), (1, 0)])]
    ppermute x23 -> x22, starting transfers between devices: 38.6 us -> 37.7 us  [permute(): return lax.ppermute(array, AXES, moves(target))]
  transfers between devices with their start and end apart: 36 -> 35, of which waited for: 17 -> 17; matrix products, arithmetic and copies ran while one was open for 8% -> 5% of each run, Pallas kernels for 0% -> 3%
where the time goes in v4:
time: 192 us; the launch traced here: 191 us
  waiting for transfers between devices  86.4 us (45%)
  starting transfers between devices  55.4 us (29%)
  Pallas kernels  18.4 us (10%)
  blocking collectives  16.4 us (9%)
  local copies, waits for them, and re-layouts  10.6 us (6%)
  other arithmetic  3.53 us (2%)
    ppermute x22, waiting for transfers between devices, permute(): return lax.ppermute(array, AXES, moves(target))  61.1 us
    ppermute x22, starting transfers between devices, permute(): return lax.ppermute(array, AXES, moves(target))  37.7 us
    all_to_all x1, blocking collectives, body(): term = lax.all_to_all(term, ('zh', 'y'), 0, 0, tiled=True)  16.4 us
    all_to_all x1, waiting for transfers between devices, body(): lax.all_to_all(partial, ('x', 'y'), 0, 0, tiled=True).astype(F32).sum(0)  13.8 us
    pallas_call x3, Pallas kernels, body(): pl.pallas_call(functools.partial(step_kernel, k), in_specs=[SMEM] + [VMEM...  9.78 us
    pallas_call x1, Pallas kernels, partial_products(): pl.pallas_call(partial_kernel, grid=(groups,), in_specs=[pl.BlockSpec((wi...  7.91 us
    all_to_all x1, starting transfers between devices, body(): lax.all_to_all(partial, ('x', 'y'), 0, 0, tiled=True).astype(F32).sum(0)  7.56 us
    ppermute x1, waiting for transfers between devices, body(): far_source = lax.ppermute(sent_half, 'zh', [(0, 1), (1, 0)])  6.92 us
  transfers between devices with their start and end apart: 35, of which 17 were waited for; matrix products, arithmetic and copies ran while one was open for 5% of the time, Pallas kernels for 3%

profile of v4, /device:TPU:102, one launch (start us, length us, event | category | flops | bytes accessed | tf_op | source)
XLA Modules:
  0.0 191.2 jit_solution(886449181853964344)
XLA Ops:
  0.0 0.1 collective-permute-start.6
  0.1 3.7 %collective-permute-start.2 = (bf16[64,3072]{1,0:T(8,128)(2,1)}, bf16[64,3072]{1,0:T(8,128)(2,1)}, u32[]{:S(2)}, u32[]{:S(2)}) collective-permute-start(bf16[64,3072]{1,0:T(8,128)(2,1)} %bitcast.21), channel_id=1, source_target_pairs={{0,2},{2,4},{4,6},{6,0},{1,3},{3,5},{5,7},{7,1},{8,10},{10,12},{12... | collective-permute-start | bytes 1179656 | tf_op jit(solution)/shard_map/ppermute | solution.py:159
  3.8 0.7 broadcast_select_fusion
  4.6 5.0 %collective-permute-start = (bf16[32,256]{1,0:T(8,128)(2,1)S(1)}, bf16[32,256]{1,0:T(8,128)(2,1)}, u32[]{:S(2)}, u32[]{:S(2)}) collective-permute-start(bf16[32,256]{1,0:T(8,128)(2,1)S(1)} %broadcast_select_fusion), channel_id=1, source_target_pairs={{0,32},{32,0},{1,33},{33,1},{2,34},{34,2},{3,35},{35,3},{4,36},{36... | collective-permute-start | bytes 49160 | tf_op jit(solution)/shard_map/ppermute | solution.py:155
  9.6 1.1 constant_dynamic-slice_fusion.1
  10.7 0.1 collective-permute-start.8
  10.8 3.2 %fusion = (bf16[256,2048]{1,0:T(8,128)(2,1)}, bf16[256,2048]{1,0:T(8,128)(2,1)S(1)}, bf16[256,2048]{1,0:T(8,128)(2,1)S(1)}) fusion(bf16[256,8192]{1,0:T(8,128)(2,1)} %param.7), kind=kLoop, calls=%fused_computation.14 | loop fusion | bytes 6291456 | tf_op jit(solution)/shard_map/slice | solution.py:151
  14.0 19.8 %collective-permute-done.8.far_mine.refs_3_ = bf16[1024,256]{1,0:T(8,128)(2,1)S(1)} collective-permute-done((bf16[1024,256]{1,0:T(8,128)(2,1)S(1)}, bf16[1024,256]{1,0:T(8,128)(2,1)S(1)}, u32[]{:S(2)}, u32[]{:S(2)}) %collective-permute-start.8) | collective-permute-done | bytes 524320 | tf_op jit(solution)/shard_map/ppermute | solution.py:36
  33.8 2.7 %constant_dynamic-slice_fusion = (bf16[128,2048]{1,0:T(8,128)(2,1)}, bf16[128,2048]{1,0:T(8,128)(2,1)}, bf16[128,2048]{1,0:T(8,128)(2,1)}) fusion(bf16[256,8192]{1,0:T(8,128)(2,1)} %param.7, s32[]{:T(128)S(6)} %select_n.51), kind=kLoop, calls=%fused_computation.10 | loop fusion | bytes 3145732 | tf_op jit(solution)/shard_map/dynamic_slice | solution.py:147
  36.5 6.9 %collective-permute-done = bf16[32,256]{1,0:T(8,128)(2,1)} collective-permute-done((bf16[32,256]{1,0:T(8,128)(2,1)S(1)}, bf16[32,256]{1,0:T(8,128)(2,1)}, u32[]{:S(2)}, u32[]{:S(2)}) %collective-permute-start) | collective-permute-done | bytes 16416 | tf_op jit(solution)/shard_map/ppermute | solution.py:155
  43.4 0.5 collective-permute-start.7
  44.0 0.1 collective-permute-start.5
  44.1 0.4 collective-permute-start.3
  44.5 0.7 collective-permute-done.1.refs_1_
  45.2 0.8 collective-permute-done.7.refs_7_
  45.9 0.6 collective-permute-done.5.refs_5_
  46.5 0.6 collective-permute-done.3.refs_3_
  47.1 0.1 copy-done.10
  47.2 0.6 copy-done.11
  47.8 0.8 copy-done.3
  48.6 7.9 %shard_map.55 = bf16[4,4,128,256]{3,2,1,0:T(8,128)(2,1)} custom-call(bf16[64,3072]{1,0:T(8,128)(2,1)} %bitcast.22, bf16[64,3072]{1,0:T(8,128)(2,1)} %copy-done.8, bf16[64,3072]{1,0:T(8,128)(2,1)} %collective-permute-done.2.refs_2_, bf16[64,3072]{1,0:T(8,128)(2,1)} %copy-done.11, bf16[64,3072]{1,0:T(8,128)(2,1)} %collective-permute-done.4.refs_4_, ...), custom_call_target="tpu_custom_call" | custom-call | tf_op jit(solution)/shard_map/pallas_call | solution.py:78
  56.5 7.6 %all-to-all-start = ((bf16[16,128,256]{2,1,0:T(8,128)(2,1)}), bf16[16,128,256]{2,1,0:T(8,128)(2,1)}, u32[]{:S(2)}, u32[]{:S(2)}) async-start(bf16[16,128,256]{2,1,0:T(8,128)(2,1)} %bitcast.17), calls=%async_computation | async-start | bytes 2097152 | tf_op jit(solution)/shard_map/all_to_all | solution.py:169
  64.1 1.9 collective-permute-start.14
  66.0 13.8 %all-to-all-done = bf16[16,128,256]{2,1,0:T(8,128)(2,1)} async-done(((bf16[16,128,256]{2,1,0:T(8,128)(2,1)}), bf16[16,128,256]{2,1,0:T(8,128)(2,1)}, u32[]{:S(2)}, u32[]{:S(2)}) %all-to-all-start) | async-done | bytes 1048608 | tf_op jit(solution)/shard_map/all_to_all | solution.py:169
  79.8 1.4 convert_reduce_fusion
  81.3 8.0 %collective-permute-start.12 = (f32[32,256]{1,0:T(8,128)S(1)}, f32[32,256]{1,0:T(8,128)S(1)}, u32[]{:S(2)}, u32[]{:S(2)}) collective-permute-start(f32[32,256]{1,0:T(8,128)S(1)} %get-tuple-element.132), channel_id=1, source_target_pairs={{0,1},{1,0},{2,67},{3,66},{4,133},{5,132},{6,199},{7,198},{8,9},{9... | collective-permute-start | bytes 98312 | tf_op jit(solution)/shard_map/ppermute | solution.py:36
  89.3 2.1 %collective-permute-start.10 = (f32[32,256]{1,0:T(8,128)S(1)}, f32[32,256]{1,0:T(8,128)S(1)}, u32[]{:S(2)}, u32[]{:S(2)}) collective-permute-start(f32[32,256]{1,0:T(8,128)S(1)} %get-tuple-element.133), channel_id=1, source_target_pairs={{0,0},{1,1},{2,66},{3,67},{4,132},{5,133},{6,198},{7,199},{8,8},{9... | collective-permute-start | bytes 98312 | tf_op jit(solution)/shard_map/ppermute | solution.py:36
  91.4 1.9 %collective-permute-start.11 = (f32[32,256]{1,0:T(8,128)S(1)}, f32[32,256]{1,0:T(8,128)S(1)}, u32[]{:S(2)}, u32[]{:S(2)}) collective-permute-start(f32[32,256]{1,0:T(8,128)S(1)} %get-tuple-element.134), channel_id=1, source_target_pairs={{0,32},{1,33},{2,98},{3,99},{4,164},{5,165},{6,230},{7,231},{8,40}... | collective-permute-start | bytes 98312 | tf_op jit(solution)/shard_map/ppermute | solution.py:36
  93.3 0.5 collective-permute-done.14.refs_10_.refs_14_
  93.9 2.4 %collective-permute-done.10 = f32[32,256]{1,0:T(8,128)S(1)} collective-permute-done((f32[32,256]{1,0:T(8,128)S(1)}, f32[32,256]{1,0:T(8,128)S(1)}, u32[]{:S(2)}, u32[]{:S(2)}) %collective-permute-start.10) | collective-permute-done | bytes 32800 | tf_op jit(solution)/shard_map/ppermute | solution.py:36
  96.3 5.5 %collective-permute-done.11 = f32[32,256]{1,0:T(8,128)S(1)} collective-permute-done((f32[32,256]{1,0:T(8,128)S(1)}, f32[32,256]{1,0:T(8,128)S(1)}, u32[]{:S(2)}, u32[]{:S(2)}) %collective-permute-start.11) | collective-permute-done | bytes 32800 | tf_op jit(solution)/shard_map/ppermute | solution.py:36
  101.8 0.8 select_subtract_fusion
  102.6 1.0 copy-done.2
  103.6 1.0 copy-done.4
  104.7 0.7 shard_map.56
  105.4 0.7 collective-permute-start.18
  106.1 0.7 collective-permute-start.17
  106.8 0.7 collective-permute-start.16
  107.5 0.7 collective-permute-start.15
  108.3 6.8 %collective-permute-start.20 = (bf16[128,2048]{1,0:T(8,128)(2,1)}, bf16[128,2048]{1,0:T(8,128)(2,1)S(1)}, u32[]{:S(2)}, u32[]{:S(2)}) collective-permute-start(bf16[128,2048]{1,0:T(8,128)(2,1)} %get-tuple-element.97), channel_id=1, source_target_pairs={{128,160},{129,161},{130,162},{131,163},{132,164},{133,165},{134,1... | collective-permute-start | bytes 1572872 | tf_op jit(solution)/shard_map/ppermute | solution.py:36
  115.1 2.4 %shard_map.57 = (f32[32,256]{1,0:T(8,128)S(1)}, f32[32,256]{1,0:T(8,128)S(1)}, bf16[32,2048]{1,0:T(8,128)(2,1)S(1)}, bf16[32,2048]{1,0:T(8,128)(2,1)S(1)}) custom-call(s32[1]{0:T(128)} %bitcast.core_ref, f32[32,256]{1,0:T(8,128)S(1)} %get-tuple-element.130.near.refs_0_, f32[32,256]{1,0:T(8,128)S(1)} %get-tuple-element.129.far.refs_1_, ...), custom_call_target="tpu_custom_call" | custom-call | tf_op jit(solution)/shard_map/pallas_call | solution.py:219
  117.5 0.8 collective-permute-start.24
  118.3 0.7 collective-permute-start.23
  119.0 0.7 collective-permute-start.22
  119.7 0.7 collective-permute-start.21
  120.4 0.7 collective-permute-start.25
  121.1 17.8 %collective-permute-done.20.refs_10_.refs_17_ = bf16[128,2048]{1,0:T(8,128)(2,1)S(1)} collective-permute-done((bf16[128,2048]{1,0:T(8,128)(2,1)}, bf16[128,2048]{1,0:T(8,128)(2,1)S(1)}, u32[]{:S(2)}, u32[]{:S(2)}) %collective-permute-start.20) | collective-permute-done | bytes 524320 | tf_op jit(solution)/shard_map/ppermute | solution.py:36
  138.9 0.1 collective-permute-start.26
  139.0 4.2 %collective-permute-start.27 = (bf16[128,2048]{1,0:T(8,128)(2,1)S(1)}, bf16[128,2048]{1,0:T(8,128)(2,1)S(1)}, u32[]{:S(2)}, u32[]{:S(2)}) collective-permute-start(bf16[128,2048]{1,0:T(8,128)(2,1)S(1)} %copy-done.6), channel_id=1, source_target_pairs={{192,224},{193,225},{194,226},{195,227},{196,228},{197,229},{198,2... | collective-permute-start | bytes 1572872 | tf_op jit(solution)/shard_map/ppermute | solution.py:36
  143.3 3.0 %shard_map.58 = (f32[32,256]{1,0:T(8,128)S(1)}, f32[32,256]{1,0:T(8,128)S(1)}, bf16[32,4096]{1,0:T(8,128)(2,1)S(1)}, bf16[32,2048]{1,0:T(8,128)(2,1)S(1)}) custom-call(s32[1]{0:T(128)} %bitcast.core_ref, f32[32,256]{1,0:T(8,128)S(1)} %get-tuple-element.95.refs_0_, f32[32,256]{1,0:T(8,128)S(1)} %get-tuple-element.96.refs_1_, bf16[2048,256]{1,0:T(8,128)(2,1)S(1)} %copy-done, ...), custom_call_target="tpu_custom_call" | custom-call | tf_op jit(solution)/shard_map/pallas_call | solution.py:219
  146.3 1.3 collective-permute-start.31
  147.6 1.3 collective-permute-start.30
  148.9 1.3 collective-permute-start.29
  150.2 1.3 collective-permute-start.28
  151.5 5.8 %collective-permute-done.31.refs_12_ = bf16[32,4096]{1,0:T(8,128)(2,1)S(1)} collective-permute-done((bf16[32,4096]{1,0:T(8,128)(2,1)S(1)}, bf16[32,4096]{1,0:T(8,128)(2,1)S(1)}, u32[]{:S(2)}, u32[]{:S(2)}) %collective-permute-start.31) | collective-permute-done | bytes 262176 | tf_op jit(solution)/shard_map/ppermute | solution.py:36
  157.4 1.3 collective-permute-start.32
  158.7 4.3 %collective-permute-done.27.refs_10_ = bf16[128,2048]{1,0:T(8,128)(2,1)S(1)} collective-permute-done((bf16[128,2048]{1,0:T(8,128)(2,1)S(1)}, bf16[128,2048]{1,0:T(8,128)(2,1)S(1)}, u32[]{:S(2)}, u32[]{:S(2)}) %collective-permute-start.27) | collective-permute-done | bytes 524320 | tf_op jit(solution)/shard_map/ppermute | solution.py:36
  163.0 1.9 collective-permute-done.29.refs_6_
  164.9 2.0 %collective-permute-done.28.refs_5_ = bf16[32,2048]{1,0:T(8,128)(2,1)S(1)} collective-permute-done((bf16[32,2048]{1,0:T(8,128)(2,1)S(1)}, bf16[32,2048]{1,0:T(8,128)(2,1)S(1)}, u32[]{:S(2)}, u32[]{:S(2)}) %collective-permute-start.28) | collective-permute-done | bytes 131104 | tf_op jit(solution)/shard_map/ppermute | solution.py:36
  166.9 0.9 collective-permute-done.32.refs_8_
  167.9 1.9 collective-permute-done.33.refs_11_
  169.8 4.3 %shard_map.59 = (f32[32,256]{1,0:T(8,128)}, f32[32,256]{1,0:T(8,128)}, bf16[32,6144]{1,0:T(8,128)(2,1)}, bf16[32,2048]{1,0:T(8,128)(2,1)S(1)}) custom-call(s32[1]{0:T(128)} %bitcast.core_ref, f32[32,256]{1,0:T(8,128)S(1)} %get-tuple-element.108.refs_0_, f32[32,256]{1,0:T(8,128)S(1)} %get-tuple-element.109.refs_1_, bf16[2048,256]{1,0:T(8,128)(2,1)S(1)} %copy-done, ...), custom_call_target="tpu_custom_call" | custom-call | tf_op jit(solution)/shard_map/pallas_call | solution.py:219
  174.1 16.4 %all_to_all.10 = bf16[8,32,256]{2,1,0:T(8,128)(2,1)S(1)} all-to-all(bf16[8,32,256]{2,1,0:T(8,128)(2,1)S(1)} %bitcast.18), channel_id=1, replica_groups=mesh['x'=4,'zh'=2,'y'=4,'zl'=4,'core'=2] {'zh','y'}, dimensions={0} | all-to-all | bytes 262144 | tf_op jit(solution)/shard_map/all_to_all | solution.py:239
  190.5 0.6 bitcast_reduce_fusion
  (45 shorter events, 0.3 us)
Async XLA Ops:
  0.0 43.4 %collective-permute-start.6 = (bf16[64,3072]{1,0:T(8,128)(2,1)}, bf16[64,3072]{1,0:T(8,128)(2,1)}, u32[]{:S(2)}, u32[]{:S(2)}) collective-permute-start(bf16[64,3072]{1,0:T(8,128)(2,1)} %bitcast.19), channel_id=1, source_target_pairs={{0,6},{2,0},{4,2},{6,4},{1,7},{3,1},{5,3},{7,5},{8,14},{10,8},{12,... | collective-permute-start | bytes 1179656 | tf_op jit(solution)/shard_map/ppermute | solution.py:159
  0.1 43.8 %collective-permute-start.4 = (bf16[64,3072]{1,0:T(8,128)(2,1)}, bf16[64,3072]{1,0:T(8,128)(2,1)}, u32[]{:S(2)}, u32[]{:S(2)}) collective-permute-start(bf16[64,3072]{1,0:T(8,128)(2,1)} %bitcast.20), channel_id=1, source_target_pairs={{0,4},{2,6},{4,0},{6,2},{1,5},{3,7},{5,1},{7,3},{8,12},{10,14},{12... | collective-permute-start | bytes 1179656 | tf_op jit(solution)/shard_map/ppermute | solution.py:159
  0.1 43.9 %collective-permute-start.2 = (bf16[64,3072]{1,0:T(8,128)(2,1)}, bf16[64,3072]{1,0:T(8,128)(2,1)}, u32[]{:S(2)}, u32[]{:S(2)}) collective-permute-start(bf16[64,3072]{1,0:T(8,128)(2,1)} %bitcast.21), channel_id=1, source_target_pairs={{0,2},{2,4},{4,6},{6,0},{1,3},{3,5},{5,7},{7,1},{8,10},{10,12},{12... | collective-permute-start | bytes 1179656 | tf_op jit(solution)/shard_map/ppermute | solution.py:159
  4.6 38.9 %collective-permute-start = (bf16[32,256]{1,0:T(8,128)(2,1)S(1)}, bf16[32,256]{1,0:T(8,128)(2,1)}, u32[]{:S(2)}, u32[]{:S(2)}) collective-permute-start(bf16[32,256]{1,0:T(8,128)(2,1)S(1)} %broadcast_select_fusion), channel_id=1, source_target_pairs={{0,32},{32,0},{1,33},{33,1},{2,34},{34,2},{3,35},{35,3},{4,36},{36... | collective-permute-start | bytes 49160 | tf_op jit(solution)/shard_map/ppermute | solution.py:155
  10.7 32.7 %copy-start.7 = (bf16[3072,64]{0,1:T(8,128)(2,1)S(1)}, bf16[3072,64]{0,1:T(8,128)(2,1)}, u32[]{:S(2)}) copy-start(bf16[3072,64]{0,1:T(8,128)(2,1)} %param.6) | copy-start | bytes 1179652
  10.7 23.1 %collective-permute-start.8 = (bf16[1024,256]{1,0:T(8,128)(2,1)S(1)}, bf16[1024,256]{1,0:T(8,128)(2,1)S(1)}, u32[]{:S(2)}, u32[]{:S(2)}) collective-permute-start(bf16[1024,256]{1,0:T(8,128)(2,1)S(1)} %constant_dynamic-slice_fusion.1), channel_id=1, source_target_pairs={{0,38},{1,39},{2,36},{3,37},{4,34},{5,35},{6,32},{7,33},{8,46},{9,... | collective-permute-start | bytes 1572872 | tf_op jit(solution)/shard_map/ppermute | solution.py:36
  33.8 13.3 %copy-start.1 = (bf16[1024,256]{1,0:T(8,128)(2,1)}, bf16[1024,256]{1,0:T(8,128)(2,1)S(1)}, u32[]{:S(2)}) copy-start(bf16[1024,256]{1,0:T(8,128)(2,1)S(1)} %collective-permute-done.8.far_mine.refs_3_) | copy-start | bytes 1572868
  33.8 13.3 %collective-permute-start.9 = (bf16[1024,256]{1,0:T(8,128)(2,1)S(1)}, bf16[1024,256]{1,0:T(8,128)(2,1)S(1)}, u32[]{:S(2)}, u32[]{:S(2)}) collective-permute-start(bf16[1024,256]{1,0:T(8,128)(2,1)S(1)} %collective-permute-done.8.far_mine.refs_3_), channel_id=1, source_target_pairs={{0,1},{1,0},{2,3},{3,2},{4,5},{5,4},{6,7},{7,6},{8,9},{9,8},{10,11... | collective-permute-start | bytes 1572872 | tf_op jit(solution)/shard_map/ppermute | solution.py:40
  43.4 1.7 collective-permute-start.1
  43.4 2.5 %collective-permute-start.7 = (bf16[64,3072]{1,0:T(8,128)(2,1)}, bf16[64,3072]{1,0:T(8,128)(2,1)S(1)}, u32[]{:S(2)}, u32[]{:S(2)}) collective-permute-start(bf16[64,3072]{1,0:T(8,128)(2,1)} %collective-permute-done.6.refs_6_), channel_id=1, source_target_pairs={{0,1},{1,0},{2,3},{3,2},{4,5},{5,4},{6,7},{7,6},{8,9},{9,8},{10,11... | collective-permute-start | bytes 1179656 | tf_op jit(solution)/shard_map/ppermute | solution.py:40
  44.0 2.5 %collective-permute-start.5 = (bf16[64,3072]{1,0:T(8,128)(2,1)}, bf16[64,3072]{1,0:T(8,128)(2,1)S(1)}, u32[]{:S(2)}, u32[]{:S(2)}) collective-permute-start(bf16[64,3072]{1,0:T(8,128)(2,1)} %collective-permute-done.4.refs_4_), channel_id=1, source_target_pairs={{0,1},{1,0},{2,3},{3,2},{4,5},{5,4},{6,7},{7,6},{8,9},{9,8},{10,11... | collective-permute-start | bytes 1179656 | tf_op jit(solution)/shard_map/ppermute | solution.py:40
  44.1 3.0 %collective-permute-start.3 = (bf16[64,3072]{1,0:T(8,128)(2,1)}, bf16[64,3072]{1,0:T(8,128)(2,1)S(1)}, u32[]{:S(2)}, u32[]{:S(2)}) collective-permute-start(bf16[64,3072]{1,0:T(8,128)(2,1)} %collective-permute-done.2.refs_2_), channel_id=1, source_target_pairs={{0,1},{1,0},{2,3},{3,2},{4,5},{5,4},{6,7},{7,6},{8,9},{9,8},{10,11... | collective-permute-start | bytes 1179656 | tf_op jit(solution)/shard_map/ppermute | solution.py:40
  45.2 1.9 copy-start.8
  45.9 1.1 copy-start.9
  46.5 0.7 copy-start.10
  47.1 0.8 copy-start.11
  47.8 0.8 copy-start.3
  56.5 46.1 %copy-start = (bf16[2048,256]{1,0:T(8,128)(2,1)S(1)}, bf16[2048,256]{1,0:T(8,128)(2,1)}, u32[]{:S(2)}) copy-start(bf16[2048,256]{1,0:T(8,128)(2,1)} %refs_2_.5) | copy-start | bytes 3145732
  56.5 23.3 %all-to-all-start = ((bf16[16,128,256]{2,1,0:T(8,128)(2,1)}), bf16[16,128,256]{2,1,0:T(8,128)(2,1)}, u32[]{:S(2)}, u32[]{:S(2)}) async-start(bf16[16,128,256]{2,1,0:T(8,128)(2,1)} %bitcast.17), calls=%async_computation | async-start | bytes 2097152 | tf_op jit(solution)/shard_map/all_to_all | solution.py:169
  64.1 29.8 %collective-permute-start.14 = (bf16[128,2048]{1,0:T(8,128)(2,1)}, bf16[128,2048]{1,0:T(8,128)(2,1)}, u32[]{:S(2)}, u32[]{:S(2)}) collective-permute-start(bf16[128,2048]{1,0:T(8,128)(2,1)} %get-tuple-element.76), channel_id=1, source_target_pairs={{64,102},{65,103},{66,100},{67,101},{68,98},{69,99},{70,96},{71,97... | collective-permute-start | bytes 1572872 | tf_op jit(solution)/shard_map/ppermute | solution.py:36
  81.2 12.7 %collective-permute-start.13 = (f32[32,256]{1,0:T(8,128)S(1)}, f32[32,256]{1,0:T(8,128)S(1)}, u32[]{:S(2)}, u32[]{:S(2)}) collective-permute-start(f32[32,256]{1,0:T(8,128)S(1)} %get-tuple-element.131), channel_id=1, source_target_pairs={{0,33},{1,32},{2,99},{3,98},{4,165},{5,164},{6,231},{7,230},{8,41}... | collective-permute-start | bytes 98312 | tf_op jit(solution)/shard_map/ppermute | solution.py:36
  81.3 12.6 %collective-permute-start.12 = (f32[32,256]{1,0:T(8,128)S(1)}, f32[32,256]{1,0:T(8,128)S(1)}, u32[]{:S(2)}, u32[]{:S(2)}) collective-permute-start(f32[32,256]{1,0:T(8,128)S(1)} %get-tuple-element.132), channel_id=1, source_target_pairs={{0,1},{1,0},{2,67},{3,66},{4,133},{5,132},{6,199},{7,198},{8,9},{9... | collective-permute-start | bytes 98312 | tf_op jit(solution)/shard_map/ppermute | solution.py:36
  89.3 7.0 %collective-permute-start.10 = (f32[32,256]{1,0:T(8,128)S(1)}, f32[32,256]{1,0:T(8,128)S(1)}, u32[]{:S(2)}, u32[]{:S(2)}) collective-permute-start(f32[32,256]{1,0:T(8,128)S(1)} %get-tuple-element.133), channel_id=1, source_target_pairs={{0,0},{1,1},{2,66},{3,67},{4,132},{5,133},{6,198},{7,199},{8,8},{9... | collective-permute-start | bytes 98312 | tf_op jit(solution)/shard_map/ppermute | solution.py:36
  91.4 10.4 %collective-permute-start.11 = (f32[32,256]{1,0:T(8,128)S(1)}, f32[32,256]{1,0:T(8,128)S(1)}, u32[]{:S(2)}, u32[]{:S(2)}) collective-permute-start(f32[32,256]{1,0:T(8,128)S(1)} %get-tuple-element.134), channel_id=1, source_target_pairs={{0,32},{1,33},{2,98},{3,99},{4,164},{5,165},{6,230},{7,231},{8,40}... | collective-permute-start | bytes 98312 | tf_op jit(solution)/shard_map/ppermute | solution.py:36
  102.6 1.0 copy-start.2
  103.6 1.0 copy-start.4
  104.7 34.3 %copy-start.6 = (bf16[128,2048]{1,0:T(8,128)(2,1)S(1)}, bf16[128,2048]{1,0:T(8,128)(2,1)}, u32[]{:S(2)}) copy-start(bf16[128,2048]{1,0:T(8,128)(2,1)} %get-tuple-element.111) | copy-start | bytes 1572868
  105.4 2.7 %collective-permute-start.18 = (bf16[32,2048]{1,0:T(8,128)(2,1)S(1)}, bf16[32,2048]{1,0:T(8,128)(2,1)S(1)}, u32[]{:S(2)}, u32[]{:S(2)}) collective-permute-start(bf16[32,2048]{1,0:T(8,128)(2,1)S(1)} %shard_map.56), channel_id=1, source_target_pairs={{0,64},{1,65},{2,66},{3,67},{4,68},{5,69},{6,70},{7,71},{8,72},{9,... | collective-permute-start | bytes 393224 | tf_op jit(solution)/shard_map/ppermute | solution.py:36
  106.1 2.0 %collective-permute-start.17 = (bf16[32,2048]{1,0:T(8,128)(2,1)S(1)}, bf16[32,2048]{1,0:T(8,128)(2,1)S(1)}, u32[]{:S(2)}, u32[]{:S(2)}) collective-permute-start(bf16[32,2048]{1,0:T(8,128)(2,1)S(1)} %shard_map.56), channel_id=1, source_target_pairs={{0,88},{1,89},{2,90},{3,91},{4,92},{5,93},{6,94},{7,95},{8,64},{9,... | collective-permute-start | bytes 393224 | tf_op jit(solution)/shard_map/ppermute | solution.py:36
  106.8 1.4 collective-permute-start.16
  107.5 0.7 collective-permute-start.15
  108.2 6.9 %collective-permute-start.19 = (bf16[128,2048]{1,0:T(8,128)(2,1)}, bf16[128,2048]{1,0:T(8,128)(2,1)S(1)}, u32[]{:S(2)}, u32[]{:S(2)}) collective-permute-start(bf16[128,2048]{1,0:T(8,128)(2,1)} %collective-permute-done.14.refs_10_.refs_14_), channel_id=1, source_target_pairs={{0,1},{1,0},{2,3},{3,2},{4,5},{5,4},{6,7},{7,6},{8,9},{9,8},{10,11... | collective-permute-start | bytes 1572872 | tf_op jit(solution)/shard_map/ppermute | solution.py:40
  108.3 30.6 %collective-permute-start.20 = (bf16[128,2048]{1,0:T(8,128)(2,1)}, bf16[128,2048]{1,0:T(8,128)(2,1)S(1)}, u32[]{:S(2)}, u32[]{:S(2)}) collective-permute-start(bf16[128,2048]{1,0:T(8,128)(2,1)} %get-tuple-element.97), channel_id=1, source_target_pairs={{128,160},{129,161},{130,162},{131,163},{132,164},{133,165},{134,1... | collective-permute-start | bytes 1572872 | tf_op jit(solution)/shard_map/ppermute | solution.py:36
  117.5 52.3 %copy-start.5 = (bf16[256,2048]{1,0:T(8,128)(2,1)S(1)}, bf16[256,2048]{1,0:T(8,128)(2,1)}, u32[]{:S(2)}) copy-start(bf16[256,2048]{1,0:T(8,128)(2,1)} %get-tuple-element.119.refs_9_) | copy-start | bytes 3145732
  117.5 2.8 %collective-permute-start.24 = (bf16[32,2048]{1,0:T(8,128)(2,1)S(1)}, bf16[32,2048]{1,0:T(8,128)(2,1)S(1)}, u32[]{:S(2)}, u32[]{:S(2)}) collective-permute-start(bf16[32,2048]{1,0:T(8,128)(2,1)S(1)} %get-tuple-element.99), channel_id=1, source_target_pairs={{64,128},{65,129},{66,130},{67,131},{68,132},{69,133},{70,134},{71... | collective-permute-start | bytes 393224 | tf_op jit(solution)/shard_map/ppermute | solution.py:36
  118.3 20.5 %collective-permute-start.23 = (bf16[32,2048]{1,0:T(8,128)(2,1)S(1)}, bf16[32,2048]{1,0:T(8,128)(2,1)S(1)}, u32[]{:S(2)}, u32[]{:S(2)}) collective-permute-start(bf16[32,2048]{1,0:T(8,128)(2,1)S(1)} %get-tuple-element.100), channel_id=1, source_target_pairs={{64,152},{65,153},{66,154},{67,155},{68,156},{69,157},{70,158},{71... | collective-permute-start | bytes 393224 | tf_op jit(solution)/shard_map/ppermute | solution.py:36
  119.0 19.9 %collective-permute-start.22 = (bf16[32,2048]{1,0:T(8,128)(2,1)S(1)}, bf16[32,2048]{1,0:T(8,128)(2,1)S(1)}, u32[]{:S(2)}, u32[]{:S(2)}) collective-permute-start(bf16[32,2048]{1,0:T(8,128)(2,1)S(1)} %get-tuple-element.100), channel_id=1, source_target_pairs={{64,144},{65,145},{66,146},{67,147},{68,148},{69,149},{70,150},{71... | collective-permute-start | bytes 393224 | tf_op jit(solution)/shard_map/ppermute | solution.py:36
  119.7 19.2 %collective-permute-start.21 = (bf16[32,2048]{1,0:T(8,128)(2,1)S(1)}, bf16[32,2048]{1,0:T(8,128)(2,1)S(1)}, u32[]{:S(2)}, u32[]{:S(2)}) collective-permute-start(bf16[32,2048]{1,0:T(8,128)(2,1)S(1)} %get-tuple-element.100), channel_id=1, source_target_pairs={{64,136},{65,137},{66,138},{67,139},{68,140},{69,141},{70,142},{71... | collective-permute-start | bytes 393224 | tf_op jit(solution)/shard_map/ppermute | solution.py:36
  120.4 18.5 %collective-permute-start.25 = (bf16[32,2048]{1,0:T(8,128)(2,1)S(1)}, bf16[32,2048]{1,0:T(8,128)(2,1)S(1)}, u32[]{:S(2)}, u32[]{:S(2)}) collective-permute-start(bf16[32,2048]{1,0:T(8,128)(2,1)S(1)} %get-tuple-element.100), channel_id=1, source_target_pairs={{64,128},{65,129},{66,130},{67,131},{68,132},{69,133},{70,134},{71... | collective-permute-start | bytes 393224 | tf_op jit(solution)/shard_map/ppermute | solution.py:36
  138.9 4.4 %collective-permute-start.26 = (bf16[128,2048]{1,0:T(8,128)(2,1)S(1)}, bf16[128,2048]{1,0:T(8,128)(2,1)S(1)}, u32[]{:S(2)}, u32[]{:S(2)}) collective-permute-start(bf16[128,2048]{1,0:T(8,128)(2,1)S(1)} %collective-permute-done.20.refs_10_.refs_17_), channel_id=1, source_target_pairs={{0,1},{1,0},{2,3},{3,2},{4,5},{5,4},{6,7},{7,6},{8,9},{9,8},{10,11... | collective-permute-start | bytes 1572872 | tf_op jit(solution)/shard_map/ppermute | solution.py:40
  139.0 24.0 %collective-permute-start.27 = (bf16[128,2048]{1,0:T(8,128)(2,1)S(1)}, bf16[128,2048]{1,0:T(8,128)(2,1)S(1)}, u32[]{:S(2)}, u32[]{:S(2)}) collective-permute-start(bf16[128,2048]{1,0:T(8,128)(2,1)S(1)} %copy-done.6), channel_id=1, source_target_pairs={{192,224},{193,225},{194,226},{195,227},{196,228},{197,229},{198,2... | collective-permute-start | bytes 1572872 | tf_op jit(solution)/shard_map/ppermute | solution.py:36
  146.3 11.0 %collective-permute-start.31 = (bf16[32,4096]{1,0:T(8,128)(2,1)S(1)}, bf16[32,4096]{1,0:T(8,128)(2,1)S(1)}, u32[]{:S(2)}, u32[]{:S(2)}) collective-permute-start(bf16[32,4096]{1,0:T(8,128)(2,1)S(1)} %get-tuple-element.113), channel_id=1, source_target_pairs={{128,192},{129,193},{130,194},{131,195},{132,196},{133,197},{134,1... | collective-permute-start | bytes 786440 | tf_op jit(solution)/shard_map/ppermute | solution.py:36
  147.6 15.4 %collective-permute-start.30 = (bf16[32,2048]{1,0:T(8,128)(2,1)S(1)}, bf16[32,2048]{1,0:T(8,128)(2,1)S(1)}, u32[]{:S(2)}, u32[]{:S(2)}) collective-permute-start(bf16[32,2048]{1,0:T(8,128)(2,1)S(1)} %get-tuple-element.114), channel_id=1, source_target_pairs={{128,216},{129,217},{130,218},{131,219},{132,220},{133,221},{134,2... | collective-permute-start | bytes 393224 | tf_op jit(solution)/shard_map/ppermute | solution.py:36
  148.9 16.0 %collective-permute-start.29 = (bf16[32,2048]{1,0:T(8,128)(2,1)S(1)}, bf16[32,2048]{1,0:T(8,128)(2,1)S(1)}, u32[]{:S(2)}, u32[]{:S(2)}) collective-permute-start(bf16[32,2048]{1,0:T(8,128)(2,1)S(1)} %get-tuple-element.114), channel_id=1, source_target_pairs={{128,208},{129,209},{130,210},{131,211},{132,212},{133,213},{134,2... | collective-permute-start | bytes 393224 | tf_op jit(solution)/shard_map/ppermute | solution.py:36
  150.2 16.7 %collective-permute-start.28 = (bf16[32,2048]{1,0:T(8,128)(2,1)S(1)}, bf16[32,2048]{1,0:T(8,128)(2,1)S(1)}, u32[]{:S(2)}, u32[]{:S(2)}) collective-permute-start(bf16[32,2048]{1,0:T(8,128)(2,1)S(1)} %get-tuple-element.114), channel_id=1, source_target_pairs={{128,200},{129,201},{130,202},{131,203},{132,204},{133,205},{134,2... | collective-permute-start | bytes 393224 | tf_op jit(solution)/shard_map/ppermute | solution.py:36
  157.4 10.5 %collective-permute-start.32 = (bf16[32,2048]{1,0:T(8,128)(2,1)S(1)}, bf16[32,2048]{1,0:T(8,128)(2,1)S(1)}, u32[]{:S(2)}, u32[]{:S(2)}) collective-permute-start(bf16[32,2048]{1,0:T(8,128)(2,1)S(1)} %get-tuple-element.114), channel_id=1, source_target_pairs={{128,192},{129,193},{130,194},{131,195},{132,196},{133,197},{134,1... | collective-permute-start | bytes 393224 | tf_op jit(solution)/shard_map/ppermute | solution.py:36
  167.9 1.9 collective-permute-start.33
